TPU v7x, 1024 devices: a whole 4x4x32 slice. The times are simulated.
1024 devices in a mesh: slab: 64 (over x_lo, z), blk: 16 (over x_hi, y, core).
Axes of the slice: x: 4 (x_hi: 2, x_lo: 2; x = x_hi * 2 + x_lo), y: 4, z: 32, core: 2. Of those that a mesh axis runs over, the one named last changes fastest.
Arguments:
- density: float32 [256, 256, 128], P('slab', 'blk'), may hold values from 0.05 to 1
- solid: int32 [256, 256, 128], P('slab', 'blk'), may hold values 0 or 1
- load: float32 [3, 256, 256, 128], P(None, 'slab', 'blk'), may hold values from -6 to 6
- start: float32 [3, 256, 256, 128], P(None, 'slab', 'blk'), may hold values from -4.5 to 7
- stencil: float32 [27, 3, 3], replicated, as said below
- owner: int32 [64, 16, 64, 1], P('slab', 'blk'), may hold values from 0 to 15; in each aligned block of 64 rows (0 to 63, 64 to 127, ..., all dimensions but the last counted through in order) at most 10 rows name the same one
Outputs:
- displacement: float32 [3, 256, 256, 128], P(None, 'slab', 'blk')
- owned: float32 [64, 16, 16, 10, 128], P('slab', 'blk')
Inputs may be any that keep to these rules, and one draw needn't show every extreme that they name: Among the 64 blocks of one device no owner is named more than 10 times, a bound that some block reaches. For every row a of every offset block the stencil's center entry stencil[13, a, a] exceeds the sum of the magnitudes of all other entries of row a over all offsets.
All inputs are finite; a program needn't handle non-finite values. No bound on the sum of `solid` on one device may be relied on, other than what follows from the above.
Results may differ from a plain program's by a relative error of at most 0.0001.
Values sent between devices are 32-bit elements; how exact they have to be, the bound alone decides.
A program may use at most 32 MiB of HBM per device.

v0:
```python
import jax
import jax.numpy as jnp
from jax import lax
from jax.sharding import PartitionSpec as P

BLOCK = 128


WEIGHTS = (1.0, 2.0, 3.0, 4.0, 5.0, 4.0, 3.0, 2.0, 1.0)
OMEGA = 0.6
EMIN = 0.1
PENAL = 3.0


def padded_2(value, sides, width):
    for axis, dim in sides:
        devices, length = (lax.axis_size(axis), value.shape[dim])
        up = [(i, (i + 1) % devices) for i in range(devices - 1)]
        down = [(j, i) for i, j in up]
        last = lax.slice_in_dim(value, length - width, length, axis=dim)
        first = lax.slice_in_dim(value, 0, width, axis=dim)
        before = lax.ppermute(last, axis, up)
        after = lax.ppermute(first, axis, down)
        value = jnp.concatenate([before, value, after], axis=dim)
    return value


def smooth_axis(padded, axis, count):
    result = WEIGHTS[0] * lax.slice_in_dim(padded, 0, count, axis=axis)
    for shift in range(1, 9):
        result = result + WEIGHTS[shift] * lax.slice_in_dim(padded, shift, shift + count, axis=axis)
    return result


def design_filter(field):
    rows, cols, depth = field.shape
    padded = padded_2(field, (("slab", 0), ("blk", 1)), 4)
    padded = jnp.pad(padded, ((0, 0), (0, 0), (4, 4)))
    padded = smooth_axis(padded, 0, rows)
    padded = smooth_axis(padded, 1, cols)
    return smooth_axis(padded, 2, depth)


def edge_weights(first_pos, count, extent):
    places = first_pos + jnp.arange(count, dtype=jnp.int32)
    result = jnp.zeros((count,), jnp.float32)
    for shift in range(9):
        target = places + (shift - 4)
        inside = jnp.logical_and(target >= 0, target < extent)
        result = result + WEIGHTS[shift] * inside.astype(jnp.float32)
    return result


def stencil_sum(padded, stencil):
    rows = padded.shape[1] - 2
    cols = padded.shape[2] - 2
    depth = padded.shape[3] - 2
    result = None
    for step_x in range(3):
        views = []
        for step_y in range(3):
            for step_z in range(3):
                views.append(
                    padded[
                        :, step_x : step_x + rows, step_y : step_y + cols, step_z : step_z + depth
                    ]
                )
        stacked = jnp.stack(views).reshape(27, rows * cols * depth)
        coeffs = stencil[9 * step_x : 9 * step_x + 9].transpose(1, 0, 2).reshape(3, 27)
        contrib = jnp.dot(
            coeffs, stacked, precision=lax.Precision.HIGHEST, preferred_element_type=jnp.float32
        )
        result = contrib if result is None else result + contrib
    return result.reshape(3, rows, cols, depth)


def apply_operator(field, stencil):
    padded = padded_2(field, (("slab", 1), ("blk", 2)), 1)
    padded = jnp.pad(padded, ((0, 0), (0, 0), (0, 0), (1, 1)))
    return stencil_sum(padded, stencil)


def restrict(field):
    lead = field.shape[0]
    rows, cols, depth = field.shape[1:]
    shaped = field.reshape(lead, rows // 2, 2, cols // 2, 2, depth // 2, 2)
    return jnp.mean(shaped, axis=(2, 4, 6))


def prolong(field):
    field = jnp.repeat(field, 2, axis=1)
    field = jnp.repeat(field, 2, axis=2)
    return jnp.repeat(field, 2, axis=3)


def deliver(filtered, owner):
    groups = lax.axis_size("blk")
    per_dev = owner.shape[2]
    slots = min(per_dev, per_dev * 5 // (2 * groups))
    blocks = filtered.reshape(per_dev, BLOCK)
    names = owner.reshape(per_dev)
    own_index = lax.axis_index("blk").astype(jnp.float32)
    data = lax.all_gather(blocks[None], "blk", axis=0, tiled=True)
    labels = lax.all_gather(names.astype(jnp.float32)[None], "blk", axis=0, tiled=True)
    count = data.shape[0]
    mine = labels == own_index
    rank = jnp.cumsum(mine.astype(jnp.int32), axis=1) - 1
    target = jnp.where(mine, rank, slots)
    row_idx = jnp.arange(count, dtype=jnp.int32)[:, None]
    placed = (
        jnp.zeros((count, slots, BLOCK), jnp.float32).at[row_idx, target].set(data, mode="drop")
    )
    return placed[None, None]


def on_device(density, solid, load, start, stencil, owner):
    rows, cols, depth = density.shape
    extent_x = rows * lax.axis_size("slab")
    extent_y = cols * lax.axis_size("blk")
    weight_x = edge_weights(lax.axis_index("slab") * rows, rows, extent_x)
    weight_y = edge_weights(lax.axis_index("blk") * cols, cols, extent_y)
    weight_z = edge_weights(jnp.int32(0), depth, depth)
    weight_sum = weight_x[:, None, None] * weight_y[None, :, None] * weight_z[None, None, :]
    xphys = design_filter(density) / weight_sum
    solid_field = solid.astype(jnp.float32)
    young = EMIN + solid_field * (xphys * xphys * xphys)
    center_diag = jnp.diagonal(stencil[13])[:, None, None, None]
    scale = young[None] * center_diag
    first = start + OMEGA * (load - young[None] * apply_operator(start, stencil)) / scale
    resid = load - young[None] * apply_operator(first, stencil)
    coarse_resid = restrict(resid)
    coarse_young = restrict(young[None])[0]
    coarse_scale = coarse_young[None] * center_diag
    corr_one = OMEGA * coarse_resid / coarse_scale
    corr_two = (
        corr_one
        + OMEGA
        * (coarse_resid - coarse_young[None] * apply_operator(corr_one, stencil))
        / coarse_scale
    )
    displacement = first + prolong(corr_two)
    energy = jnp.sum(displacement * apply_operator(displacement, stencil), axis=0)
    sens = -PENAL * xphys * xphys * solid_field * energy
    filtered = design_filter(density * sens) / (weight_sum * density)
    return (displacement, deliver(filtered, owner))


def solution(mesh):
    placed = (
        P("slab", "blk", None),
        P("slab", "blk", None),
        P(None, "slab", "blk", None),
        P(None, "slab", "blk", None),
        P(),
        P("slab", "blk", None, None),
    )
    return jax.shard_map(
        on_device,
        mesh=mesh,
        in_specs=placed,
        out_specs=(P(None, "slab", "blk", None), P("slab", "blk", None, None, None)),
        check_vma=False,
    )
```

profile of v0, /device:TPU:7, one launch (start us, length us, event | category | flops | bytes accessed | tf_op | source)
XLA Modules:
  0.0 236.3 jit_solution(6536596812241192503)
XLA Ops:
  0.6 18.7 %collective-permute-start.1 = (f32[4,16,128]{2,1,0:T(8,128)}, f32[4,16,128]{2,1,0:T(8,128)S(1)}, u32[]{:S(2)}, u32[]{:S(2)}) collective-permute-start(f32[4,16,128]{2,1,0:T(8,128)} %param.6), channel_id=1, source_target_pairs={{16,0},{32,16},{48,32},{64,48},{80,64},{96,80},{112,96},{128,112},... | collective-permute-start | bytes 98312 | tf_op jit(solution)/shard_map/ppermute | solution.py:23
  19.3 1.9 collective-permute-start
  21.2 0.8 fusion.110
  22.0 5.5 %collective-permute-start.5 = (f32[3,1,16,128]{3,2,1,0:T(8,128)S(1)}, f32[3,1,16,128]{3,2,1,0:T(8,128)S(1)}, u32[]{:S(2)}, u32[]{:S(2)}) collective-permute-start(f32[3,1,16,128]{3,2,1,0:T(8,128)S(1)} %get-tuple-element.135), channel_id=1, source_target_pairs={{16,0},{32,16},{48,32},{64,48},{80,64},{96,80},{112,96},{128,112},... | collective-permute-start | bytes 73736 | tf_op jit(solution)/shard_map/ppermute | solution.py:23
  27.5 1.9 collective-permute-start.4
  30.0 0.8 slice_reduce_fusion
  30.8 0.9 slice_bitcast_fusion.84
  32.4 1.2 gather_fusion
  34.2 0.9 constant_dynamic-update-slice_fusion.4
  35.1 5.8 %collective-permute-start.6 = (f32[3,6,1,128]{3,2,1,0:T(1,128)S(1)}, f32[3,6,1,128]{3,2,1,0:T(1,128)S(1)}, u32[]{:S(2)}, u32[]{:S(2)}) collective-permute-start(f32[3,6,1,128]{3,2,1,0:T(1,128)S(1)} %get-tuple-element.98), channel_id=1, source_target_pairs={{0,1},{1,2},{2,3},{3,4},{4,5},{5,6},{6,7},{7,8},{8,9},{9,10},{10,1... | collective-permute-start | bytes 27656 | tf_op jit(solution)/shard_map/ppermute | solution.py:22
  40.9 1.9 collective-permute-start.7
  42.8 0.8 constant_dynamic-update-slice_fusion.1
  44.2 3.6 %collective-permute-start.2 = (f32[12,4,128]{2,1,0:T(4,128)}, f32[12,4,128]{2,1,0:T(4,128)S(1)}, u32[]{:S(2)}, u32[]{:S(2)}) collective-permute-start(f32[12,4,128]{2,1,0:T(4,128)} %get-tuple-element.130), channel_id=1, source_target_pairs={{0,1},{1,2},{2,3},{3,4},{4,5},{5,6},{6,7},{7,8},{8,9},{9,10},{10,1... | collective-permute-start | bytes 73736 | tf_op jit(solution)/shard_map/ppermute | solution.py:22
  47.8 4.4 %collective-permute-start.3 = (f32[12,4,128]{2,1,0:T(4,128)}, f32[12,4,128]{2,1,0:T(4,128)S(1)}, u32[]{:S(2)}, u32[]{:S(2)}) collective-permute-start(f32[12,4,128]{2,1,0:T(4,128)} %get-tuple-element.131), channel_id=1, source_target_pairs={{1,0},{2,1},{3,2},{4,3},{5,4},{6,5},{7,6},{8,7},{9,8},{10,9},{11,1... | collective-permute-start | bytes 73736 | tf_op jit(solution)/shard_map/ppermute | solution.py:23
  55.2 1.7 constant_dynamic-update-slice_fusion.28
  56.9 0.8 constant_dynamic-update-slice_fusion.27
  60.1 1.3 reshape.319
  64.0 0.8 fusion.55
  65.5 1.9 collective-permute-start.8
  67.5 5.5 %collective-permute-start.9 = (f32[3,1,16,128]{3,2,1,0:T(8,128)S(1)}, f32[3,1,16,128]{3,2,1,0:T(8,128)S(1)}, u32[]{:S(2)}, u32[]{:S(2)}) collective-permute-start(f32[3,1,16,128]{3,2,1,0:T(8,128)S(1)} %get-tuple-element.129), channel_id=1, source_target_pairs={{16,0},{32,16},{48,32},{64,48},{80,64},{96,80},{112,96},{128,112},... | collective-permute-start | bytes 73736 | tf_op jit(solution)/shard_map/ppermute | solution.py:23
  72.9 2.1 reshape_broadcast_in_dim.3
  75.3 1.9 collective-permute-start.10
  77.3 8.0 %collective-permute-start.11 = (f32[3,6,1,128]{3,2,1,0:T(1,128)S(1)}, f32[3,6,1,128]{3,2,1,0:T(1,128)S(1)}, u32[]{:S(2)}, u32[]{:S(2)}) collective-permute-start(f32[3,6,1,128]{3,2,1,0:T(1,128)S(1)} %get-tuple-element.97), channel_id=1, source_target_pairs={{1,0},{2,1},{3,2},{4,3},{5,4},{6,5},{7,6},{8,7},{9,8},{10,9},{11,1... | collective-permute-start | bytes 27656 | tf_op jit(solution)/shard_map/ppermute | solution.py:23
  87.6 0.8 constant_dynamic-update-slice_fusion.61
  89.7 0.8 constant_dynamic-update-slice_fusion.58
  92.8 1.3 reshape.326
  96.4 7.7 %reshape.330 = f32[3,2,2,8,2,64,2]{6,5,4,3,2,1,0:T(8,128)} reshape(f32[3,4,16,128]{3,2,1,0:T(8,128)S(1)} %multiply_subtract_fusion) | data formatting | bytes 196608 | tf_op jit(solution)/shard_map/reshape | solution.py:86
  104.1 3.3 %reduce_sum.27 = f32[3,2,8,64]{3,2,1,0:T(8,128)S(1)} reduce(f32[3,2,2,8,2,64,2]{6,5,4,3,2,1,0:T(8,128)} %reshape.330, f32[]{:T(128)} %constant.36.clone.1), dimensions={2,4,6}, to_apply=%region_0.1 | reduce | flops 21504 | bytes 110596 | tf_op jit(solution)/shard_map/reduce_sum | solution.py:87
  107.5 1.9 collective-permute-start.12
  109.4 5.5 %collective-permute-start.13 = (f32[3,1,8,64]{3,2,1,0:T(8,128)S(1)}, f32[3,1,8,64]{3,2,1,0:T(8,128)S(1)}, u32[]{:S(2)}, u32[]{:S(2)}) collective-permute-start(f32[3,1,8,64]{3,2,1,0:T(8,128)S(1)} %get-tuple-element.148), channel_id=1, source_target_pairs={{16,0},{32,16},{48,32},{64,48},{80,64},{96,80},{112,96},{128,112},... | collective-permute-start | bytes 18440 | tf_op jit(solution)/shard_map/ppermute | solution.py:23
  114.9 26.5 %all-gather = f32[16,1,64,1]{2,3,1,0:T(1,128)S(1)} all-gather(f32[1,1,64,1]{2,3,1,0:T(1,128)S(1)} %convert_element_type.101), channel_id=2, replica_groups=mesh['slab'=64,'blk'=16] {'blk'}, dimensions={0}, use_global_device_ids=true | all-gather | bytes 4352 | tf_op jit(solution)/shard_map/all_gather | solution.py:104
  141.4 2.3 collective-permute-start.14
  143.7 2.0 collective-permute-start.15
  146.0 3.0 %collective-permute-done.15 = f32[3,4,1,64]{3,2,1,0:T(1,128)S(1)} collective-permute-done((f32[3,4,1,64]{3,2,1,0:T(1,128)S(1)}, f32[3,4,1,64]{3,2,1,0:T(1,128)S(1)}, u32[]{:S(2)}, u32[]{:S(2)}) %collective-permute-start.15) | collective-permute-done | bytes 3104 | tf_op jit(solution)/shard_map/ppermute | solution.py:23
  151.5 1.9 collective-permute-start.16
  153.4 5.5 %collective-permute-start.17 = (f32[3,1,16,128]{3,2,1,0:T(8,128)S(1)}, f32[3,1,16,128]{3,2,1,0:T(8,128)S(1)}, u32[]{:S(2)}, u32[]{:S(2)}) collective-permute-start(f32[3,1,16,128]{3,2,1,0:T(8,128)S(1)} %get-tuple-element.106), channel_id=1, source_target_pairs={{16,0},{32,16},{48,32},{64,48},{80,64},{96,80},{112,96},{128,112},... | collective-permute-start | bytes 73736 | tf_op jit(solution)/shard_map/ppermute | solution.py:23
  158.9 0.9 collective-permute-done.17
  159.8 2.8 %collective-permute-start.18 = (f32[3,6,1,128]{3,2,1,0:T(1,128)S(1)}, f32[3,6,1,128]{3,2,1,0:T(1,128)S(1)}, u32[]{:S(2)}, u32[]{:S(2)}) collective-permute-start(f32[3,6,1,128]{3,2,1,0:T(1,128)S(1)} %get-tuple-element.92), channel_id=1, source_target_pairs={{0,1},{1,2},{2,3},{3,4},{4,5},{5,6},{6,7},{7,8},{8,9},{9,10},{10,1... | collective-permute-start | bytes 27656 | tf_op jit(solution)/shard_map/ppermute | solution.py:22
  162.7 5.4 %collective-permute-start.19 = (f32[3,6,1,128]{3,2,1,0:T(1,128)S(1)}, f32[3,6,1,128]{3,2,1,0:T(1,128)S(1)}, u32[]{:S(2)}, u32[]{:S(2)}) collective-permute-start(f32[3,6,1,128]{3,2,1,0:T(1,128)S(1)} %get-tuple-element.93), channel_id=1, source_target_pairs={{1,0},{2,1},{3,2},{4,3},{5,4},{6,5},{7,6},{8,7},{9,8},{10,9},{11,1... | collective-permute-start | bytes 27656 | tf_op jit(solution)/shard_map/ppermute | solution.py:23
  172.8 0.8 constant_dynamic-update-slice_fusion.116
  175.9 1.3 reshape.338
  179.5 6.0 %collective-permute-start.21 = (f32[4,16,128]{2,1,0:T(8,128)S(1)}, f32[4,16,128]{2,1,0:T(8,128)S(1)}, u32[]{:S(2)}, u32[]{:S(2)}) collective-permute-start(f32[4,16,128]{2,1,0:T(8,128)S(1)} %fusion.58), channel_id=1, source_target_pairs={{16,0},{32,16},{48,32},{64,48},{80,64},{96,80},{112,96},{128,112},... | collective-permute-start | bytes 98312 | tf_op jit(solution)/shard_map/ppermute | solution.py:23
  185.5 1.9 collective-permute-start.20
  187.6 4.9 %collective-permute-done.20 = f32[4,16,128]{2,1,0:T(8,128)S(1)} collective-permute-done((f32[4,16,128]{2,1,0:T(8,128)S(1)}, f32[4,16,128]{2,1,0:T(8,128)S(1)}, u32[]{:S(2)}, u32[]{:S(2)}) %collective-permute-start.20) | collective-permute-done | bytes 32800 | tf_op jit(solution)/shard_map/ppermute | solution.py:22
  192.4 2.0 collective-permute-start.22
  194.4 9.0 %collective-permute-start.23 = (f32[12,4,128]{2,1,0:T(4,128)S(1)}, f32[12,4,128]{2,1,0:T(4,128)S(1)}, u32[]{:S(2)}, u32[]{:S(2)}) collective-permute-start(f32[12,4,128]{2,1,0:T(4,128)S(1)} %get-tuple-element.101), channel_id=1, source_target_pairs={{1,0},{2,1},{3,2},{4,3},{5,4},{6,5},{7,6},{8,7},{9,8},{10,9},{11,1... | collective-permute-start | bytes 73736 | tf_op jit(solution)/shard_map/ppermute | solution.py:23
  204.8 27.9 %all_gather.7 = f32[16,64,128]{2,1,0:T(8,128)S(1)} all-gather(f32[1,64,128]{2,1,0:T(8,128)S(1)} %bitcast.501), channel_id=1, replica_groups=mesh['slab'=64,'blk'=16] {'blk'}, dimensions={0}, use_global_device_ids=true | all-gather | bytes 557056 | tf_op jit(solution)/shard_map/all_gather | solution.py:103
  232.7 3.7 %scatter_custom_fusion = f32[160,128]{1,0:T(8,128)} fusion(s32[1024]{0:T(1024)S(1)} %reshape.352, f32[1024,128]{1,0:T(8,128)S(1)} %bitcast.495, f32[]{:T(128)} %constant.36.clone.1), kind=kCustom, calls=%fused_computation.332 | custom fusion | bytes 81924
  (175 shorter events, 32.8 us)
Async XLA Ops:
  0.6 42.9 %collective-permute-start.1 = (f32[4,16,128]{2,1,0:T(8,128)}, f32[4,16,128]{2,1,0:T(8,128)S(1)}, u32[]{:S(2)}, u32[]{:S(2)}) collective-permute-start(f32[4,16,128]{2,1,0:T(8,128)} %param.6), channel_id=1, source_target_pairs={{16,0},{32,16},{48,32},{64,48},{80,64},{96,80},{112,96},{128,112},... | collective-permute-start | bytes 98312 | tf_op jit(solution)/shard_map/ppermute | solution.py:23
  19.3 23.5 %collective-permute-start = (f32[4,16,128]{2,1,0:T(8,128)}, f32[4,16,128]{2,1,0:T(8,128)S(1)}, u32[]{:S(2)}, u32[]{:S(2)}) collective-permute-start(f32[4,16,128]{2,1,0:T(8,128)} %param.6), channel_id=1, source_target_pairs={{0,16},{16,32},{32,48},{48,64},{64,80},{80,96},{96,112},{112,128},... | collective-permute-start | bytes 98312 | tf_op jit(solution)/shard_map/ppermute | solution.py:22
  22.0 13.1 %collective-permute-start.5 = (f32[3,1,16,128]{3,2,1,0:T(8,128)S(1)}, f32[3,1,16,128]{3,2,1,0:T(8,128)S(1)}, u32[]{:S(2)}, u32[]{:S(2)}) collective-permute-start(f32[3,1,16,128]{3,2,1,0:T(8,128)S(1)} %get-tuple-element.135), channel_id=1, source_target_pairs={{16,0},{32,16},{48,32},{64,48},{80,64},{96,80},{112,96},{128,112},... | collective-permute-start | bytes 73736 | tf_op jit(solution)/shard_map/ppermute | solution.py:23
  27.5 6.7 %collective-permute-start.4 = (f32[3,1,16,128]{3,2,1,0:T(8,128)S(1)}, f32[3,1,16,128]{3,2,1,0:T(8,128)S(1)}, u32[]{:S(2)}, u32[]{:S(2)}) collective-permute-start(f32[3,1,16,128]{3,2,1,0:T(8,128)S(1)} %get-tuple-element.136), channel_id=1, source_target_pairs={{0,16},{16,32},{32,48},{48,64},{64,80},{80,96},{96,112},{112,128},... | collective-permute-start | bytes 73736 | tf_op jit(solution)/shard_map/ppermute | solution.py:22
  35.1 17.1 %collective-permute-start.6 = (f32[3,6,1,128]{3,2,1,0:T(1,128)S(1)}, f32[3,6,1,128]{3,2,1,0:T(1,128)S(1)}, u32[]{:S(2)}, u32[]{:S(2)}) collective-permute-start(f32[3,6,1,128]{3,2,1,0:T(1,128)S(1)} %get-tuple-element.98), channel_id=1, source_target_pairs={{0,1},{1,2},{2,3},{3,4},{4,5},{5,6},{6,7},{7,8},{8,9},{9,10},{10,1... | collective-permute-start | bytes 27656 | tf_op jit(solution)/shard_map/ppermute | solution.py:22
  40.9 11.4 %collective-permute-start.7 = (f32[3,6,1,128]{3,2,1,0:T(1,128)S(1)}, f32[3,6,1,128]{3,2,1,0:T(1,128)S(1)}, u32[]{:S(2)}, u32[]{:S(2)}) collective-permute-start(f32[3,6,1,128]{3,2,1,0:T(1,128)S(1)} %get-tuple-element.99), channel_id=1, source_target_pairs={{1,0},{2,1},{3,2},{4,3},{5,4},{6,5},{7,6},{8,7},{9,8},{10,9},{11,1... | collective-permute-start | bytes 27656 | tf_op jit(solution)/shard_map/ppermute | solution.py:23
  44.2 19.4 %collective-permute-start.2 = (f32[12,4,128]{2,1,0:T(4,128)}, f32[12,4,128]{2,1,0:T(4,128)S(1)}, u32[]{:S(2)}, u32[]{:S(2)}) collective-permute-start(f32[12,4,128]{2,1,0:T(4,128)} %get-tuple-element.130), channel_id=1, source_target_pairs={{0,1},{1,2},{2,3},{3,4},{4,5},{5,6},{6,7},{7,8},{8,9},{9,10},{10,1... | collective-permute-start | bytes 73736 | tf_op jit(solution)/shard_map/ppermute | solution.py:22
  47.8 15.8 %collective-permute-start.3 = (f32[12,4,128]{2,1,0:T(4,128)}, f32[12,4,128]{2,1,0:T(4,128)S(1)}, u32[]{:S(2)}, u32[]{:S(2)}) collective-permute-start(f32[12,4,128]{2,1,0:T(4,128)} %get-tuple-element.131), channel_id=1, source_target_pairs={{1,0},{2,1},{3,2},{4,3},{5,4},{6,5},{7,6},{8,7},{9,8},{10,9},{11,1... | collective-permute-start | bytes 73736 | tf_op jit(solution)/shard_map/ppermute | solution.py:23
  59.0 4.9 %copy-start.4 = (s32[4,16,128]{2,1,0:T(8,128)S(1)}, s32[4,16,128]{2,1,0:T(8,128)}, u32[]{:S(2)}) copy-start(s32[4,16,128]{2,1,0:T(8,128)} %param.7) | copy-start | bytes 98308
  59.8 5.0 %copy-start.1 = (f32[3,4,16,128]{3,2,1,0:T(8,128)S(1)}, f32[3,4,16,128]{3,2,1,0:T(8,128)}, u32[]{:S(2)}) copy-start(f32[3,4,16,128]{3,2,1,0:T(8,128)} %param.9) | copy-start | bytes 294916
  59.8 5.0 %copy-start.2 = (f32[3,4,16,128]{3,2,1,0:T(8,128)S(1)}, f32[3,4,16,128]{3,2,1,0:T(8,128)}, u32[]{:S(2)}) copy-start(f32[3,4,16,128]{3,2,1,0:T(8,128)} %param.8) | copy-start | bytes 294916
  65.5 9.7 %collective-permute-start.8 = (f32[3,1,16,128]{3,2,1,0:T(8,128)S(1)}, f32[3,1,16,128]{3,2,1,0:T(8,128)S(1)}, u32[]{:S(2)}, u32[]{:S(2)}) collective-permute-start(f32[3,1,16,128]{3,2,1,0:T(8,128)S(1)} %get-tuple-element.128), channel_id=1, source_target_pairs={{0,16},{16,32},{32,48},{48,64},{64,80},{80,96},{96,112},{112,128},... | collective-permute-start | bytes 73736 | tf_op jit(solution)/shard_map/ppermute | solution.py:22
  67.5 7.8 %collective-permute-start.9 = (f32[3,1,16,128]{3,2,1,0:T(8,128)S(1)}, f32[3,1,16,128]{3,2,1,0:T(8,128)S(1)}, u32[]{:S(2)}, u32[]{:S(2)}) collective-permute-start(f32[3,1,16,128]{3,2,1,0:T(8,128)S(1)} %get-tuple-element.129), channel_id=1, source_target_pairs={{16,0},{32,16},{48,32},{64,48},{80,64},{96,80},{112,96},{128,112},... | collective-permute-start | bytes 73736 | tf_op jit(solution)/shard_map/ppermute | solution.py:23
  75.3 9.9 %collective-permute-start.10 = (f32[3,6,1,128]{3,2,1,0:T(1,128)S(1)}, f32[3,6,1,128]{3,2,1,0:T(1,128)S(1)}, u32[]{:S(2)}, u32[]{:S(2)}) collective-permute-start(f32[3,6,1,128]{3,2,1,0:T(1,128)S(1)} %get-tuple-element.96), channel_id=1, source_target_pairs={{0,1},{1,2},{2,3},{3,4},{4,5},{5,6},{6,7},{7,8},{8,9},{9,10},{10,1... | collective-permute-start | bytes 27656 | tf_op jit(solution)/shard_map/ppermute | solution.py:22
  77.3 8.6 %collective-permute-start.11 = (f32[3,6,1,128]{3,2,1,0:T(1,128)S(1)}, f32[3,6,1,128]{3,2,1,0:T(1,128)S(1)}, u32[]{:S(2)}, u32[]{:S(2)}) collective-permute-start(f32[3,6,1,128]{3,2,1,0:T(1,128)S(1)} %get-tuple-element.97), channel_id=1, source_target_pairs={{1,0},{2,1},{3,2},{4,3},{5,4},{6,5},{7,6},{8,7},{9,8},{10,9},{11,1... | collective-permute-start | bytes 27656 | tf_op jit(solution)/shard_map/ppermute | solution.py:23
  96.4 11.0 %copy-start.5 = (f32[3]{0:T(128)S(1)}, f32[3]{0:T(128)}, u32[]{:S(2)}) copy-start(f32[3]{0:T(128)} %gather_fusion) | copy-start | bytes 40
  96.4 18.5 %copy-start.9 = (s32[1,1,64,1]{2,3,1,0:T(1,128)S(1)}, s32[1,1,64,1]{2,3,1,0:T(1,128)}, u32[]{:S(2)}) copy-start(s32[1,1,64,1]{2,3,1,0:T(1,128)} %param.11) | copy-start | bytes 772
  104.1 58.6 %copy-start.8 = (s32[2]{0:T(128)S(1)}, s32[2]{0:T(128)}, u32[]{:S(2)}) copy-start(s32[2]{0:T(128)} %constant.159) | copy-start | bytes 28
  107.5 33.9 %collective-permute-start.12 = (f32[3,1,8,64]{3,2,1,0:T(8,128)S(1)}, f32[3,1,8,64]{3,2,1,0:T(8,128)S(1)}, u32[]{:S(2)}, u32[]{:S(2)}) collective-permute-start(f32[3,1,8,64]{3,2,1,0:T(8,128)S(1)} %get-tuple-element.147), channel_id=1, source_target_pairs={{0,16},{16,32},{32,48},{48,64},{64,80},{80,96},{96,112},{112,128},... | collective-permute-start | bytes 18440 | tf_op jit(solution)/shard_map/ppermute | solution.py:22
  109.4 32.0 %collective-permute-start.13 = (f32[3,1,8,64]{3,2,1,0:T(8,128)S(1)}, f32[3,1,8,64]{3,2,1,0:T(8,128)S(1)}, u32[]{:S(2)}, u32[]{:S(2)}) collective-permute-start(f32[3,1,8,64]{3,2,1,0:T(8,128)S(1)} %get-tuple-element.148), channel_id=1, source_target_pairs={{16,0},{32,16},{48,32},{64,48},{80,64},{96,80},{112,96},{128,112},... | collective-permute-start | bytes 18440 | tf_op jit(solution)/shard_map/ppermute | solution.py:23
  141.4 4.6 %collective-permute-start.14 = (f32[3,4,1,64]{3,2,1,0:T(1,128)S(1)}, f32[3,4,1,64]{3,2,1,0:T(1,128)S(1)}, u32[]{:S(2)}, u32[]{:S(2)}) collective-permute-start(f32[3,4,1,64]{3,2,1,0:T(1,128)S(1)} %get-tuple-element.143), channel_id=1, source_target_pairs={{0,1},{1,2},{2,3},{3,4},{4,5},{5,6},{6,7},{7,8},{8,9},{9,10},{10,1... | collective-permute-start | bytes 9224 | tf_op jit(solution)/shard_map/ppermute | solution.py:22
  143.7 5.2 %collective-permute-start.15 = (f32[3,4,1,64]{3,2,1,0:T(1,128)S(1)}, f32[3,4,1,64]{3,2,1,0:T(1,128)S(1)}, u32[]{:S(2)}, u32[]{:S(2)}) collective-permute-start(f32[3,4,1,64]{3,2,1,0:T(1,128)S(1)} %get-tuple-element.144), channel_id=1, source_target_pairs={{1,0},{2,1},{3,2},{4,3},{5,4},{6,5},{7,6},{8,7},{9,8},{10,9},{11,1... | collective-permute-start | bytes 9224 | tf_op jit(solution)/shard_map/ppermute | solution.py:23
  151.5 28.0 %copy-start = (f32[3,4,16,128]{3,2,1,0:T(8,128)}, f32[3,4,16,128]{3,2,1,0:T(8,128)S(1)}, u32[]{:S(2)}) copy-start(f32[3,4,16,128]{3,2,1,0:T(8,128)S(1)} %add.698) | copy-start | bytes 294916
  151.5 7.4 %collective-permute-start.16 = (f32[3,1,16,128]{3,2,1,0:T(8,128)S(1)}, f32[3,1,16,128]{3,2,1,0:T(8,128)S(1)}, u32[]{:S(2)}, u32[]{:S(2)}) collective-permute-start(f32[3,1,16,128]{3,2,1,0:T(8,128)S(1)} %get-tuple-element.105), channel_id=1, source_target_pairs={{0,16},{16,32},{32,48},{48,64},{64,80},{80,96},{96,112},{112,128},... | collective-permute-start | bytes 73736 | tf_op jit(solution)/shard_map/ppermute | solution.py:22
  153.4 6.4 %collective-permute-start.17 = (f32[3,1,16,128]{3,2,1,0:T(8,128)S(1)}, f32[3,1,16,128]{3,2,1,0:T(8,128)S(1)}, u32[]{:S(2)}, u32[]{:S(2)}) collective-permute-start(f32[3,1,16,128]{3,2,1,0:T(8,128)S(1)} %get-tuple-element.106), channel_id=1, source_target_pairs={{16,0},{32,16},{48,32},{64,48},{80,64},{96,80},{112,96},{128,112},... | collective-permute-start | bytes 73736 | tf_op jit(solution)/shard_map/ppermute | solution.py:23
  159.8 8.3 %collective-permute-start.18 = (f32[3,6,1,128]{3,2,1,0:T(1,128)S(1)}, f32[3,6,1,128]{3,2,1,0:T(1,128)S(1)}, u32[]{:S(2)}, u32[]{:S(2)}) collective-permute-start(f32[3,6,1,128]{3,2,1,0:T(1,128)S(1)} %get-tuple-element.92), channel_id=1, source_target_pairs={{0,1},{1,2},{2,3},{3,4},{4,5},{5,6},{6,7},{7,8},{8,9},{9,10},{10,1... | collective-permute-start | bytes 27656 | tf_op jit(solution)/shard_map/ppermute | solution.py:22
  162.7 6.2 %collective-permute-start.19 = (f32[3,6,1,128]{3,2,1,0:T(1,128)S(1)}, f32[3,6,1,128]{3,2,1,0:T(1,128)S(1)}, u32[]{:S(2)}, u32[]{:S(2)}) collective-permute-start(f32[3,6,1,128]{3,2,1,0:T(1,128)S(1)} %get-tuple-element.93), channel_id=1, source_target_pairs={{1,0},{2,1},{3,2},{4,3},{5,4},{6,5},{7,6},{8,7},{9,8},{10,9},{11,1... | collective-permute-start | bytes 27656 | tf_op jit(solution)/shard_map/ppermute | solution.py:23
  172.8 6.7 %copy-start.3 = (f32[4,16,128]{2,1,0:T(8,128)S(1)}, f32[4,16,128]{2,1,0:T(8,128)}, u32[]{:S(2)}) copy-start(f32[4,16,128]{2,1,0:T(8,128)} %param.6) | copy-start | bytes 98308
  172.8 14.7 %copy-start.7 = (s32[2]{0:T(128)S(1)}, s32[2]{0:T(128)}, u32[]{:S(2)}) copy-start(s32[2]{0:T(128)} %constant.156) | copy-start | bytes 28
  175.6 29.0 %copy-start.6 = (f32[128]{0:T(128)S(1)}, f32[128]{0:T(128)}, u32[]{:S(2)}) copy-start(f32[128]{0:T(128)} %fusion.102) | copy-start | bytes 1540
  179.5 8.1 %collective-permute-start.21 = (f32[4,16,128]{2,1,0:T(8,128)S(1)}, f32[4,16,128]{2,1,0:T(8,128)S(1)}, u32[]{:S(2)}, u32[]{:S(2)}) collective-permute-start(f32[4,16,128]{2,1,0:T(8,128)S(1)} %fusion.58), channel_id=1, source_target_pairs={{16,0},{32,16},{48,32},{64,48},{80,64},{96,80},{112,96},{128,112},... | collective-permute-start | bytes 98312 | tf_op jit(solution)/shard_map/ppermute | solution.py:23
  185.5 6.9 %collective-permute-start.20 = (f32[4,16,128]{2,1,0:T(8,128)S(1)}, f32[4,16,128]{2,1,0:T(8,128)S(1)}, u32[]{:S(2)}, u32[]{:S(2)}) collective-permute-start(f32[4,16,128]{2,1,0:T(8,128)S(1)} %fusion.58), channel_id=1, source_target_pairs={{0,16},{16,32},{32,48},{48,64},{64,80},{80,96},{96,112},{112,128},... | collective-permute-start | bytes 98312 | tf_op jit(solution)/shard_map/ppermute | solution.py:22
  192.4 11.2 %collective-permute-start.22 = (f32[12,4,128]{2,1,0:T(4,128)S(1)}, f32[12,4,128]{2,1,0:T(4,128)S(1)}, u32[]{:S(2)}, u32[]{:S(2)}) collective-permute-start(f32[12,4,128]{2,1,0:T(4,128)S(1)} %get-tuple-element.100), channel_id=1, source_target_pairs={{0,1},{1,2},{2,3},{3,4},{4,5},{5,6},{6,7},{7,8},{8,9},{9,10},{10,1... | collective-permute-start | bytes 73736 | tf_op jit(solution)/shard_map/ppermute | solution.py:22
  194.4 9.9 %collective-permute-start.23 = (f32[12,4,128]{2,1,0:T(4,128)S(1)}, f32[12,4,128]{2,1,0:T(4,128)S(1)}, u32[]{:S(2)}, u32[]{:S(2)}) collective-permute-start(f32[12,4,128]{2,1,0:T(4,128)S(1)} %get-tuple-element.101), channel_id=1, source_target_pairs={{1,0},{2,1},{3,2},{4,3},{5,4},{6,5},{7,6},{8,7},{9,8},{10,9},{11,1... | collective-permute-start | bytes 73736 | tf_op jit(solution)/shard_map/ppermute | solution.py:23
where the time goes:
time: 238 us; the launch traced here: 236 us
  starting transfers between devices  107 us (45%)
  blocking collectives  54.3 us (23%)
  local copies, waits for them, and re-layouts  42.2 us (18%)
  other arithmetic  12.6 us (5%)
  waiting for transfers between devices  11.3 us (5%)
  matrix products  6.97 us (3%)
    ppermute x12, starting transfers between devices, padded_2(): after = lax.ppermute(first, axis, down)  77.3 us
    ppermute x12, starting transfers between devices, padded_2(): before = lax.ppermute(last, axis, up)  29.9 us
    all_gather x1, blocking collectives, deliver(): data = lax.all_gather(blocks[None], 'blk', axis=0, tiled=True)  27.9 us
    all_gather x1, blocking collectives, deliver(): lax.all_gather(names.astype(jnp.float32)[None], 'blk', axis=0, tiled=True)  26.5 us
    unnamed x64, local copies, waits for them, and re-layouts  19 us
    reshape x1, local copies, waits for them, and re-layouts, restrict(): shaped = field.reshape(lead, rows // 2, 2, cols // 2, 2, depth // 2, 2)  7.67 us
    dot_general x12, matrix products, stencil_sum(): jnp.dot(coeffs, stacked, precision=lax.Precision.HIGHEST, preferred_eleme...  6.97 us
    ppermute x12, waiting for transfers between devices, padded_2(): after = lax.ppermute(first, axis, down)  5.92 us
  transfers between devices with their start and end apart: 24, of which 7 were waited for; matrix products, arithmetic and copies ran while one was open for 9% of the time, Pallas kernels for 0%

commit v1 on v0

v1 whole, which is shorter than its diff:
```python
import functools

import jax
import jax.numpy as jnp
from jax import lax
from jax.experimental import pallas as pl
from jax.experimental.pallas import tpu as pltpu
from jax.sharding import PartitionSpec as P

OMEGA = 0.6
EMIN = 0.1
CAP = 10
MESH = pl.DeviceIdType.MESH
F32 = jnp.float32
BF16 = jnp.bfloat16
DIRS = ((1, 0), (-1, 0), (0, 1), (0, -1), (1, 1), (1, -1), (-1, 1), (-1, -1))


def iota(shape, dim):
    return lax.broadcasted_iota(jnp.int32, shape, dim)


def split2(value):
    high = value.astype(BF16).astype(F32)
    return high, value - high


def split3(value):
    high, rest = split2(value)
    mid, low = split2(rest)
    return high, mid, low


def lane_mod(lanes, size, count):
    for step in range(count, 0, -1):
        lanes = jnp.where(lanes >= size * step, lanes - size * step, lanes)
    return lanes


def band_position(window, wide, has_low, has_high):
    far = jnp.int32(-1000)
    low_off = jnp.where(has_low, jnp.int32(-16 - wide), far)
    high_off = jnp.where(has_high, jnp.int32(-wide), far)
    outside = jnp.where(window < 16 + wide, window + low_off, window + high_off)
    outside = jnp.where(window >= 16 + 2 * wide, far, outside)
    return jnp.where(window < 16, window, outside)


def band_matrix(st_ref, ex, rows_y, rows, wide, dilate, flags, scale, centre):
    lanes = iota((rows, 216), 1)
    window = lane_mod(lanes, 24, 8)
    position = band_position(window, wide, *flags)
    target = rows_y(iota((rows, 216), 0))
    masks = [position == target + dilate * (ey - 1) for ey in range(3)]
    lane_row = iota((1, 216), 1)
    in_comp = lane_mod(lane_row, 72, 2)
    first_comp, second_comp = in_comp < 24, in_comp < 48
    use_high = lanes < 144
    blocks = []
    for ez in range(3):
        for a in range(3):
            total = jnp.zeros((rows, 216), F32)
            for ey in range(3):
                off = 9 * ex + 3 * ey + ez
                coef = jnp.where(
                    first_comp,
                    st_ref[a, 0, off],
                    jnp.where(second_comp, st_ref[a, 1, off], st_ref[a, 2, off]),
                )
                if scale is not None:
                    coef = coef * scale[a]
                    if off == 13:
                        own = (in_comp >= 24 * a) & (in_comp < 24 * a + 24)
                        coef = coef + jnp.where(own, F32(centre), F32(0.0))
                total = jnp.where(masks[ey], coef, total)
            high, low = split2(total)
            blocks.append(jnp.where(use_high, high, low))
    return jnp.concatenate(blocks, axis=0).astype(BF16)


def stencil_apply(planes, mat_ref, rows, dilate):
    parts = []
    for plane in planes:
        high, low = split2(plane)
        parts.append(jnp.concatenate([high, low, high], axis=0).astype(BF16))
    total = None
    for ex in range(3):
        right = jnp.concatenate(parts[ex : ex + 4], axis=1)
        piece = jnp.dot(mat_ref[ex], right, preferred_element_type=F32)
        total = piece if total is None else total + piece
    size = 3 * rows
    lanes = iota((size, 128), 1)
    result = []
    for x in range(4):
        down, mid, up = (
            total[ez * size : (ez + 1) * size, x * 128 : (x + 1) * 128] for ez in range(3)
        )
        down = jnp.where(lanes >= dilate, pltpu.roll(down, dilate, 1), 0.0)
        up = jnp.where(lanes < 128 - dilate, pltpu.roll(up, 128 - dilate, 1), 0.0)
        result.append(mid + down + up)
    return result


def smooth(win_ref, wy_ref, wz_ref, mask_low, mask_high):
    planes = [win_ref[i] for i in range(12)]
    planes = [
        v * mask_low if i < 4 else v * mask_high if i >= 8 else v for i, v in enumerate(planes)
    ]
    sums = []
    for x in range(4):
        v = planes[x : x + 9]
        sums.append(
            (v[0] + v[8])
            + 2.0 * (v[1] + v[7])
            + 3.0 * (v[2] + v[6])
            + 4.0 * (v[3] + v[5])
            + 5.0 * v[4]
        )
    stacked = jnp.concatenate(split3(jnp.concatenate(sums, axis=1)), axis=0).astype(BF16)
    cols = jnp.dot(wy_ref[...], stacked, preferred_element_type=F32)
    cols = jnp.concatenate([cols[:, x * 128 : (x + 1) * 128] for x in range(4)], axis=0)
    pair = jnp.concatenate(split2(cols), axis=1).astype(BF16)
    return jnp.dot(pair, wz_ref[...], preferred_element_type=F32)


def edge_weight(place, extent):
    def missing(n):
        n = jnp.maximum(n, 0)
        return lax.shift_right_logical(n * (n + 1), 1)

    return (25 - missing(4 - place) - missing(5 + place - extent)).astype(F32)


def pair_sum(value, axis, size):
    index = iota(value.shape, axis)
    even = lax.rem(index, 2) == 0
    return value + jnp.where(
        even, pltpu.roll(value, size - 1, axis), pltpu.roll(value, 1, axis)
    )


def kernel(
    slabs,
    groups,
    cap,
    density,
    solid,
    load,
    start,
    st_ref,
    owner,
    disp_ref,
    owned_ref,
    dens_win,
    sens_win,
    f0,
    f1,
    coarse,
    load_v,
    solid_v,
    packed,
    mat1,
    mat2,
    wy_ref,
    wz_ref,
    pick_ref,
    local_sem,
    send_sem,
    recv_sem,
    give_sem,
    take_sem,
):
    p = lax.axis_index("slab")
    s = lax.axis_index("blk")

    def neighbour(dx, dy):
        return (lax.rem(p + dx + slabs, slabs), lax.rem(s + dy + groups, groups))

    locals_ = [
        pltpu.make_async_copy(start, f0.at[:, 1:5, 0:16], local_sem.at[0]),
        pltpu.make_async_copy(density, dens_win.at[4:8, 0:16], local_sem.at[1]),
        pltpu.make_async_copy(load, load_v, local_sem.at[2]),
        pltpu.make_async_copy(solid, solid_v, local_sem.at[3]),
    ]
    f0[:, :, 16:24] = jnp.zeros((3, 6, 8, 128), F32)
    f1[:, :, 16:24] = jnp.zeros((3, 6, 8, 128), F32)
    for copy in locals_:
        copy.start()

    barrier = pltpu.get_barrier_semaphore()
    partners = [neighbour(dx, dy) for dx, dy in DIRS if dx != 0]
    partners += [(p, lax.rem(s + d, groups)) for d in range(1, groups)]
    for partner in partners:
        pl.semaphore_signal(barrier, inc=1, device_id=partner, device_id_type=MESH)
    pl.semaphore_wait(barrier, len(partners))

    def remote(src, dst, row, i):
        return pltpu.make_async_remote_copy(
            src_ref=src,
            dst_ref=dst,
            send_sem=send_sem.at[row, i],
            recv_sem=recv_sem.at[row, i],
            device_id=neighbour(*DIRS[i]),
            device_id_type=MESH,
        )

    started = []

    def exchange(row, make):
        copies = [remote(*make(dx, dy), row, i) for i, (dx, dy) in enumerate(DIRS)]
        for copy in copies:
            copy.start()
        started.extend(copies)
        return copies

    def field_slices(src, base, dst):
        def make(dx, dy):
            sx = (base + 3, base, slice(base, base + 4))[(dx == -1) + 2 * (dx == 0)]
            tx = (0, 5, slice(1, 5))[(dx == -1) + 2 * (dx == 0)]
            sy = ((15, 16), (0, 1), (0, 16))[(dy == -1) + 2 * (dy == 0)]
            ty = ((16, 17), (17, 18), (0, 16))[(dy == -1) + 2 * (dy == 0)]
            return src.at[:, sx, sy[0] : sy[1]], dst.at[:, tx, ty[0] : ty[1]]

        return make

    def wide_slices(src, base, dst):
        def make(dx, dy):
            tx = (0, 8, 4)[(dx == -1) + 2 * (dx == 0)]
            sy = ((12, 16), (0, 4), (0, 16))[(dy == -1) + 2 * (dy == 0)]
            ty = ((16, 20), (20, 24), (0, 16))[(dy == -1) + 2 * (dy == 0)]
            return (
                src.at[base : base + 4, sy[0] : sy[1]],
                dst.at[tx : tx + 4, ty[0] : ty[1]],
            )

        return make

    def coarse_slices(dx, dy):
        tx = (0, 2, 1)[(dx == -1) + 2 * (dx == 0)]
        sy = ((12, 16), (0, 4), (0, 16))[(dy == -1) + 2 * (dy == 0)]
        ty = ((16, 20), (20, 24), (0, 16))[(dy == -1) + 2 * (dy == 0)]
        return coarse.at[:, 1, sy[0] : sy[1]], coarse.at[:, tx, ty[0] : ty[1]]

    start_in = exchange(0, field_slices(start, 0, f0))
    dens_in = exchange(1, wide_slices(density, 0, dens_win))

    flags = (s > 0, s < groups - 1)
    mask_low = jnp.where(p > 0, 1.0, 0.0).astype(F32)
    mask_high = jnp.where(p < slabs - 1, 1.0, 0.0).astype(F32)
    for ex in range(3):
        mat1[ex] = band_matrix(st_ref, ex, lambda r: r, 16, 1, 1, flags, None, 0.0)
    wy_pos = band_position(lane_mod(iota((16, 72), 1), 24, 2), 4, *flags)
    wy_ref[...] = jnp.maximum(5 - jnp.abs(wy_pos - iota((16, 72), 0)), 0).astype(F32).astype(BF16)
    wz_row = lane_mod(iota((256, 128), 0), 128, 1)
    wz_ref[...] = (
        jnp.maximum(5 - jnp.abs(wz_row - iota((256, 128), 1)), 0).astype(F32).astype(BF16)
    )
    weight_y = edge_weight(s * 16 + iota((16, 128), 0), 16 * groups)
    weight_z = edge_weight(iota((16, 128), 1), 128)
    weight_yz = weight_y * weight_z
    weight = jnp.concatenate(
        [
            weight_yz * edge_weight(jnp.full((16, 128), p * 4 + x, jnp.int32), 4 * slabs)
            for x in range(4)
        ],
        axis=0,
    )
    inv_weight = 1.0 / weight
    relax = [OMEGA / jnp.full((8, 128), st_ref[a, a, 13], F32)[0:1, :] for a in range(3)]

    names = owner[...].astype(F32)
    down, across = iota((64, 64), 0), iota((64, 64), 1)
    names_col = jnp.sum(jnp.where(down == across, names, 0.0), axis=1, keepdims=True)
    earlier = (names_col == names) & (across < down)
    rank = jnp.sum(jnp.where(earlier, 1.0, 0.0), axis=1, keepdims=True)
    code_col = names_col * 16.0 + rank
    spread = iota((64, 192), 0) == lane_mod(iota((64, 192), 1), 64, 2)
    code_row = jnp.sum(jnp.where(spread, code_col, 0.0), axis=0, keepdims=True)
    slot = iota((16 * groups, 192), 0).astype(F32)
    pick_ref[...] = jnp.where(slot == code_row, 1.0, 0.0).astype(BF16)

    def field_planes(ref):
        planes = [ref[:, j].reshape(72, 128) for j in range(6)]
        planes[0] = planes[0] * mask_low
        planes[5] = planes[5] * mask_high
        return planes

    locals_[0].wait()
    for copy in start_in:
        copy.wait_recv()
    s_start = stencil_apply(field_planes(f0), mat1, 16, 1)
    locals_[1].wait()
    locals_[2].wait()
    locals_[3].wait()
    for copy in dens_in:
        copy.wait_recv()
    xphys = smooth(dens_win, wy_ref, wz_ref, mask_low, mask_high) * inv_weight
    solid_f = solid_v[...].astype(F32).reshape(64, 128)
    young = EMIN + solid_f * (xphys * xphys * xphys)
    inv_young = 1.0 / young
    for a in range(3):
        for x in range(4):
            rows = slice(16 * x, 16 * x + 16)
            f1[a, 1 + x, 0:16] = f0[a, 1 + x, 0:16] + relax[a] * (
                load_v[a, x] * inv_young[rows] - s_start[x][16 * a : 16 * a + 16]
            )
    first_in = exchange(2, field_slices(f1, 1, f1))

    dens = dens_win[4:8, 0:16].reshape(64, 128)
    sens_scale = (-3.0 * dens) * (xphys * xphys) * solid_f
    out_scale = inv_weight / dens
    lanes16 = iota((16, 128), 1)
    even_lane = lax.rem(lanes16, 2) == 0

    def coarsen(quarter):
        halves = [
            pair_sum(pair_sum(quarter[2 * i] + quarter[2 * i + 1], 1, 128), 0, 16) * 0.125
            for i in range(2)
        ]
        return jnp.where(even_lane, halves[0], halves[1])

    coarse[3, 1, 0:16] = coarsen([young[16 * x : 16 * x + 16] for x in range(4)])

    def coarse_y(r):
        return jnp.where(r < 16, r, jnp.where(r == 16, -1, jnp.where(r == 17, 16, -5000)))

    for ex in range(3):
        tall = [-relax[a][:, 0:1] for a in range(3)]
        mat2[ex] = band_matrix(st_ref, ex, coarse_y, 24, 4, 2, flags, tall, 2.0)

    for copy in first_in:
        copy.wait_recv()
    s_first = stencil_apply(field_planes(f1), mat1, 16, 1)
    for a in range(3):
        coarse[a, 1, 0:16] = coarsen(
            [
                load_v[a, x] - young[16 * x : 16 * x + 16] * s_first[x][16 * a : 16 * a + 16]
                for x in range(4)
            ]
        )
    coarse_in = exchange(3, coarse_slices)
    for copy in coarse_in:
        copy.wait_recv()

    lanes72 = iota((24, 128), 1)
    even72 = lax.rem(lanes72, 2) == 0
    corr_planes = []
    for plane in range(3):
        inv_cy = 1.0 / coarse[3, plane]
        both = [relax[a] * (coarse[a, plane] * inv_cy) for a in range(3)]
        if plane == 0:
            both = [v * mask_low for v in both]
        if plane == 2:
            both = [v * mask_high for v in both]
        lower = [jnp.where(even72, v, pltpu.roll(v, 1, 1)) for v in both]
        upper = [jnp.where(even72, pltpu.roll(v, 127, 1), v) for v in both]
        corr_planes.append(jnp.concatenate(lower, axis=0))
        corr_planes.append(jnp.concatenate(upper, axis=0))
    corr = stencil_apply(corr_planes, mat2, 24, 2)

    disp = []
    for j, c in enumerate((0, 1, 1, 2, 2, 3)):
        disp.append(f1[:, j].reshape(72, 128) + corr[c])
    masked = [disp[0] * mask_low, *disp[1:5], disp[5] * mask_high]
    s_disp = stencil_apply(masked, mat1, 16, 1)
    for x in range(4):
        energy = None
        for a in range(3):
            term = disp[1 + x][24 * a : 24 * a + 16] * s_disp[x][16 * a : 16 * a + 16]
            energy = term if energy is None else energy + term
        sens_win[4 + x, 0:16] = sens_scale[16 * x : 16 * x + 16] * energy
    sens_in = exchange(4, wide_slices(sens_win, 4, sens_win))
    for x in range(4):
        for a in range(3):
            disp_ref[a, x] = disp[1 + x][24 * a : 24 * a + 16]
    for copy in sens_in:
        copy.wait_recv()
    filtered = smooth(sens_win, wy_ref, wz_ref, mask_low, mask_high) * out_scale

    three = jnp.concatenate(split3(filtered), axis=0).astype(BF16)
    rows = jnp.dot(pick_ref[...], three, preferred_element_type=F32)
    for j in range(groups):
        packed[j] = rows[16 * j : 16 * j + cap]
    gives = []
    for d in range(1, groups):
        target = lax.rem(s + d, groups)
        gives.append(
            pltpu.make_async_remote_copy(
                src_ref=packed.at[target],
                dst_ref=owned_ref.at[s],
                send_sem=give_sem.at[d],
                recv_sem=take_sem.at[d],
                device_id=(p, target),
                device_id_type=MESH,
            )
        )
        gives[-1].start()
    owned_ref[s] = packed[s]
    for copy in gives:
        copy.wait_recv()
    for copy in started + gives:
        copy.wait_send()


def on_device(density, solid, load, start, stencil, owner):
    slabs, groups = lax.axis_size("slab"), lax.axis_size("blk")
    cap = CAP
    hbm = pl.BlockSpec(memory_space=pltpu.HBM)
    vmem = pl.BlockSpec(memory_space=pltpu.VMEM)
    disp, owned = pl.pallas_call(
        functools.partial(kernel, slabs, groups, cap),
        out_shape=(
            jax.ShapeDtypeStruct(load.shape, F32),
            jax.ShapeDtypeStruct((groups, cap, 128), F32),
        ),
        in_specs=[hbm, hbm, hbm, hbm, pl.BlockSpec(memory_space=pltpu.SMEM), vmem],
        out_specs=(vmem, vmem),
        scratch_shapes=[
            pltpu.VMEM((12, 24, 128), F32),
            pltpu.VMEM((12, 24, 128), F32),
            pltpu.VMEM((3, 6, 24, 128), F32),
            pltpu.VMEM((3, 6, 24, 128), F32),
            pltpu.VMEM((4, 3, 24, 128), F32),
            pltpu.VMEM((3, 4, 16, 128), F32),
            pltpu.VMEM((4, 16, 128), jnp.int32),
            pltpu.VMEM((groups, cap, 128), F32),
            pltpu.VMEM((3, 144, 216), BF16),
            pltpu.VMEM((3, 216, 216), BF16),
            pltpu.VMEM((16, 72), BF16),
            pltpu.VMEM((256, 128), BF16),
            pltpu.VMEM((16 * groups, 192), BF16),
            pltpu.SemaphoreType.DMA((4,)),
            pltpu.SemaphoreType.DMA((5, 8)),
            pltpu.SemaphoreType.DMA((5, 8)),
            pltpu.SemaphoreType.DMA((groups,)),
            pltpu.SemaphoreType.DMA((groups,)),
        ],
        compiler_params=pltpu.CompilerParams(
            collective_id=0, has_side_effects=True, vmem_limit_bytes=32 * 1024 * 1024
        ),
    )(
        density,
        solid,
        load,
        start,
        stencil.transpose(1, 2, 0),
        owner.reshape(1, 64),
    )
    return disp, owned[None, None]


def solution(mesh):
    placed = (
        P("slab", "blk", None),
        P("slab", "blk", None),
        P(None, "slab", "blk", None),
        P(None, "slab", "blk", None),
        P(),
        P("slab", "blk", None, None),
    )
    return jax.shard_map(
        on_device,
        mesh=mesh,
        in_specs=placed,
        out_specs=(P(None, "slab", "blk", None), P("slab", "blk", None, None, None)),
        check_vma=False,
    )
```

time: 238 us -> 58.4 us (0.25)
  the two profiles are of different devices: /device:TPU:7 before, /device:TPU:1 now
where the time goes in v1:
time: 58.4 us; the launch traced here: 58 us
  Pallas kernels  51.4 us (88%)
  local copies, waits for them, and re-layouts  5.94 us (10%)
  between operations  0.65 us (1%)
    pallas_call x1, Pallas kernels, on_device(): pl.pallas_call(functools.partial(kernel, slabs, groups, cap), out_shape=(...  51.4 us
    unnamed x14, local copies, waits for them, and re-layouts  5.94 us

profile of v1, /device:TPU:1, one launch (start us, length us, event | category | flops | bytes accessed | tf_op | source)
XLA Modules:
  0.0 58.0 jit_solution(2577351566088946140)
XLA Ops:
  0.6 0.0 copy-start.5
  0.6 0.6 %copy-done.5 = s32[1,1,64,1]{2,3,1,0:T(1,128)S(1)} copy-done((s32[1,1,64,1]{2,3,1,0:T(1,128)S(1)}, s32[1,1,64,1]{2,3,1,0:T(1,128)}, u32[]{:S(2)}) %copy-start.5) | copy-done | bytes 280
  1.3 0.0 copy-start
  1.3 0.9 %copy-done = f32[3,4,16,128]{3,2,1,0:T(8,128)S(1)} copy-done((f32[3,4,16,128]{3,2,1,0:T(8,128)S(1)}, f32[3,4,16,128]{3,2,1,0:T(8,128)}, u32[]{:S(2)}) %copy-start) | copy-done | bytes 98328
  2.2 0.0 copy-start.1
  2.2 0.9 %copy-done.1 = f32[3,4,16,128]{3,2,1,0:T(8,128)S(1)} copy-done((f32[3,4,16,128]{3,2,1,0:T(8,128)S(1)}, f32[3,4,16,128]{3,2,1,0:T(8,128)}, u32[]{:S(2)}) %copy-start.1) | copy-done | bytes 98328
  3.1 0.0 copy-start.2
  3.1 0.8 %copy-done.2 = f32[4,16,128]{2,1,0:T(8,128)S(1)} copy-done((f32[4,16,128]{2,1,0:T(8,128)S(1)}, f32[4,16,128]{2,1,0:T(8,128)}, u32[]{:S(2)}) %copy-start.2) | copy-done | bytes 32792
  3.8 0.0 copy-start.3
  3.8 0.8 %copy-done.3 = s32[4,16,128]{2,1,0:T(8,128)S(1)} copy-done((s32[4,16,128]{2,1,0:T(8,128)S(1)}, s32[4,16,128]{2,1,0:T(8,128)}, u32[]{:S(2)}) %copy-start.3) | copy-done | bytes 32792
  4.6 0.0 copy-start.4
  4.6 0.7 %copy-done.4 = f32[27,3,3]{0,2,1:T(4,128)S(1)} copy-done((f32[27,3,3]{0,2,1:T(4,128)S(1)}, f32[27,3,3]{0,2,1:T(4,128)}, u32[]{:S(2)}) %copy-start.4) | copy-done | bytes 996
  5.3 51.4 %shard_map.77 = (f32[3,4,16,128]{3,2,1,0:T(8,128)S(1)}, f32[16,10,128]{2,1,0:T(8,128)S(1)}) custom-call(f32[4,16,128]{2,1,0:T(8,128)S(1)} %copy-done.2, s32[4,16,128]{2,1,0:T(8,128)S(1)} %copy-done.3, f32[3,4,16,128]{3,2,1,0:T(8,128)S(1)} %copy-done, f32[3,4,16,128]{3,2,1,0:T(8,128)S(1)} %copy-done.1, f32[3,3,27]{2,1,0:T(4,128)S(1)} %bitcast.4, ...), custom_call_target="tpu_custom_call" | custom-call | tf_op jit(solution)/shard_map/pallas_call | solution.py:410
  56.7 0.7 %copy.8 = f32[1,1,16,10,128]{4,2,3,1,0:T(8,128)} copy(f32[1,1,16,10,128]{4,3,2,1,0:T(8,128)S(1)} %bitcast.3) | data formatting | bytes 163840
  57.3 0.6 %copy.10 = f32[3,4,16,128]{3,2,1,0:T(8,128)} copy(f32[3,4,16,128]{3,2,1,0:T(8,128)S(1)} %get-tuple-element.10) | data formatting | bytes 196608
Async XLA Ops:
  0.6 0.7 %copy-start.5 = (s32[1,1,64,1]{2,3,1,0:T(1,128)S(1)}, s32[1,1,64,1]{2,3,1,0:T(1,128)}, u32[]{:S(2)}) copy-start(s32[1,1,64,1]{2,3,1,0:T(1,128)} %param.11) | copy-start | bytes 772
  1.3 0.9 %copy-start = (f32[3,4,16,128]{3,2,1,0:T(8,128)S(1)}, f32[3,4,16,128]{3,2,1,0:T(8,128)}, u32[]{:S(2)}) copy-start(f32[3,4,16,128]{3,2,1,0:T(8,128)} %load.1) | copy-start | bytes 294916
  2.2 0.9 %copy-start.1 = (f32[3,4,16,128]{3,2,1,0:T(8,128)S(1)}, f32[3,4,16,128]{3,2,1,0:T(8,128)}, u32[]{:S(2)}) copy-start(f32[3,4,16,128]{3,2,1,0:T(8,128)} %start.1) | copy-start | bytes 294916
  3.1 0.8 %copy-start.2 = (f32[4,16,128]{2,1,0:T(8,128)S(1)}, f32[4,16,128]{2,1,0:T(8,128)}, u32[]{:S(2)}) copy-start(f32[4,16,128]{2,1,0:T(8,128)} %density.1) | copy-start | bytes 98308
  3.8 0.8 %copy-start.3 = (s32[4,16,128]{2,1,0:T(8,128)S(1)}, s32[4,16,128]{2,1,0:T(8,128)}, u32[]{:S(2)}) copy-start(s32[4,16,128]{2,1,0:T(8,128)} %solid.1) | copy-start | bytes 98308
  4.6 0.7 %copy-start.4 = (f32[27,3,3]{0,2,1:T(4,128)S(1)}, f32[27,3,3]{0,2,1:T(4,128)}, u32[]{:S(2)}) copy-start(f32[27,3,3]{0,2,1:T(4,128)} %param.10) | copy-start | bytes 2920

commit v2 on v1

v2 whole, which is shorter than its diff:
```python
import functools

import jax
import jax.numpy as jnp
from jax import lax
from jax.experimental import pallas as pl
from jax.experimental.pallas import tpu as pltpu
from jax.sharding import PartitionSpec as P

OMEGA = 0.6
EMIN = 0.1
CAP = 10
MESH = pl.DeviceIdType.MESH
F32 = jnp.float32
BF16 = jnp.bfloat16
STAGE = 99
DIRS = ((1, 1), (1, -1), (-1, 1), (-1, -1), (0, 1), (0, -1), (1, 0), (-1, 0))
FAR = ((2, 1), (2, -1), (-2, 1), (-2, -1), (2, 0), (-2, 0))
HANDOUT = (12, 4, 11, 5, 13, 3, 10, 6, 14, 2, 9, 7, 8, 15, 1)


def iota(shape, dim):
    return lax.broadcasted_iota(jnp.int32, shape, dim)


def split2(value):
    high = value.astype(BF16).astype(F32)
    return high, value - high


def split3(value):
    high, rest = split2(value)
    mid, low = split2(rest)
    return high, mid, low


def lane_mod(lanes, size, count):
    for step in range(count, 0, -1):
        lanes = jnp.where(lanes >= size * step, lanes - size * step, lanes)
    return lanes


def band_position(window, wide, has_low, has_high):
    far = jnp.int32(-1000)
    low_off = jnp.where(has_low, jnp.int32(-16 - wide), far)
    high_off = jnp.where(has_high, jnp.int32(-wide), far)
    outside = jnp.where(window < 16 + wide, window + low_off, window + high_off)
    outside = jnp.where(window >= 16 + 2 * wide, far, outside)
    return jnp.where(window < 16, window, outside)


def band_matrix(st_ref, ex, rows_y, rows, wide, dilate, flags, scale, centre):
    lanes = iota((rows, 216), 1)
    window = lane_mod(lanes, 24, 8)
    position = band_position(window, wide, *flags)
    target = rows_y(iota((rows, 216), 0))
    masks = [position == target + dilate * (ey - 1) for ey in range(3)]
    lane_row = iota((1, 216), 1)
    in_comp = lane_mod(lane_row, 72, 2)
    first_comp, second_comp = in_comp < 24, in_comp < 48
    use_high = lanes < 144
    blocks = []
    for ez in range(3):
        for a in range(3):
            total = jnp.zeros((rows, 216), F32)
            for ey in range(3):
                off = 9 * ex + 3 * ey + ez
                coef = jnp.where(
                    first_comp,
                    st_ref[a, 0, off],
                    jnp.where(second_comp, st_ref[a, 1, off], st_ref[a, 2, off]),
                )
                if scale is not None:
                    coef = coef * scale[a]
                    if off == 13:
                        own = (in_comp >= 24 * a) & (in_comp < 24 * a + 24)
                        coef = coef + jnp.where(own, F32(centre), F32(0.0))
                total = jnp.where(masks[ey], coef, total)
            high, low = split2(total)
            blocks.append(jnp.where(use_high, high, low))
    return jnp.concatenate(blocks, axis=0).astype(BF16)


def stencil_apply(planes, mat_ref, rows, dilate):
    count = len(planes) - 2
    parts = []
    for plane in planes:
        high, low = split2(plane)
        parts.append(jnp.concatenate([high, low, high], axis=0).astype(BF16))
    total = None
    for ex in range(3):
        right = jnp.concatenate(parts[ex : ex + count], axis=1)
        piece = jnp.dot(mat_ref[ex], right, preferred_element_type=F32)
        total = piece if total is None else total + piece
    size = 3 * rows
    lanes = iota((size, 128), 1)
    result = []
    for x in range(count):
        down, mid, up = (
            total[ez * size : (ez + 1) * size, x * 128 : (x + 1) * 128] for ez in range(3)
        )
        down = jnp.where(lanes >= dilate, pltpu.roll(down, dilate, 1), 0.0)
        up = jnp.where(lanes < 128 - dilate, pltpu.roll(up, 128 - dilate, 1), 0.0)
        result.append(mid + down + up)
    return result


def smooth(planes, wy_ref, wz_ref):
    count = len(planes) - 8
    sums = []
    for x in range(count):
        v = planes[x : x + 9]
        sums.append(
            (v[0] + v[8])
            + 2.0 * (v[1] + v[7])
            + 3.0 * (v[2] + v[6])
            + 4.0 * (v[3] + v[5])
            + 5.0 * v[4]
        )
    stacked = jnp.concatenate(split3(jnp.concatenate(sums, axis=1)), axis=0).astype(BF16)
    cols = jnp.dot(wy_ref[...], stacked, preferred_element_type=F32)
    cols = jnp.concatenate([cols[:, x * 128 : (x + 1) * 128] for x in range(count)], axis=0)
    pair = jnp.concatenate(split2(cols), axis=1).astype(BF16)
    return jnp.dot(pair, wz_ref[...], preferred_element_type=F32)


def inner_and_ring(row):
    ring = jnp.where(row == 16, -1, jnp.where(row == 17, 16, -5000))
    return jnp.where(row < 16, row, ring)


def halo_planes(dx, width):
    if dx == 0:
        return 0, width, 4
    many = min(width - 4 * (abs(dx) - 1), 4)
    if dx > 0:
        return 4 - many, width - 4 * dx + 4 - many, many
    return 0, width - 4 * dx, many


def halo_rows(dy, width):
    if dy == 0:
        return 0, 0, 16
    return (16 - width, 16, width) if dy > 0 else (0, 16 + width, width)


def edge_weight(place, extent):
    def missing(n):
        n = jnp.maximum(n, 0)
        return lax.shift_right_logical(n * (n + 1), 1)

    weight = 25 - missing(4 - place) - missing(5 + place - extent)
    return jnp.maximum(weight, 1).astype(F32)


def pair_sum(value, axis, size):
    index = iota(value.shape, axis)
    even = lax.rem(index, 2) == 0
    return value + jnp.where(
        even, pltpu.roll(value, size - 1, axis), pltpu.roll(value, 1, axis)
    )


def kernel(
    slabs,
    groups,
    cap,
    density,
    solid,
    load,
    start,
    stencil,
    owner,
    disp_ref,
    owned_ref,
    st_ref,
    owner_v,
    dens_win,
    sens_win,
    f0,
    coarse,
    load_win,
    solid_win,
    packed,
    mat0,
    mat1,
    mat2,
    wy0_ref,
    wy1_ref,
    wz_ref,
    pick_ref,
    local_sem,
    send_sem,
    recv_sem,
    far_send,
    far_recv,
    give_sem,
    take_sem,
):
    p = lax.axis_index("slab")
    s = lax.axis_index("blk")

    def neighbour(dx, dy):
        return (lax.rem(p + dx + slabs, slabs), lax.rem(s + dy + groups, groups))

    partners = [neighbour(dx, dy) for dx, dy in FAR + DIRS if dx != 0]
    partners += [(p, lax.rem(s + d, groups)) for d in HANDOUT if d < groups]

    locals_ = [
        pltpu.make_async_copy(stencil, st_ref, local_sem.at[0]),
        pltpu.make_async_copy(owner, owner_v, local_sem.at[1]),
        pltpu.make_async_copy(start, f0.at[:, 2:6, 0:16], local_sem.at[2]),
        pltpu.make_async_copy(density, dens_win.at[5:9, 0:16], local_sem.at[3]),
        pltpu.make_async_copy(load, load_win.at[:, 1:5, 0:16], local_sem.at[4]),
        pltpu.make_async_copy(solid, solid_win.at[1:5, 0:16], local_sem.at[5]),
    ]
    f0[:, :, 16:24] = jnp.zeros((3, 8, 8, 128), F32)
    dens_win[:, 24:32] = jnp.zeros((14, 8, 128), F32)
    load_win[:, :, 16:24] = jnp.zeros((3, 6, 8, 128), F32)
    solid_win[:, 16:24] = jnp.zeros((6, 8, 128), jnp.int32)

    barrier = pltpu.get_barrier_semaphore()
    for partner in partners:
        pl.semaphore_signal(barrier, inc=1, device_id=partner, device_id_type=MESH)
    for copy in locals_:
        copy.start()
    pl.semaphore_wait(barrier, len(partners))

    started = []

    def window(src, dst, width, lead, base=0):
        def make(dx, dy):
            sx, tx, nx = halo_planes(dx, width)
            sy, ty, ny = halo_rows(dy, width)
            here = (pl.ds(base + sx, nx), pl.ds(sy, ny))
            there = (pl.ds(tx, nx), pl.ds(ty, ny))
            if lead:
                here, there = (slice(None), *here), (slice(None), *there)
            return src.at[here], dst.at[there]

        return make

    def coarse_window(fields):
        def make(dx, dy):
            sy, ty, ny = halo_rows(dy, 4)
            return (
                coarse.at[fields, 1, pl.ds(sy, ny)],
                coarse.at[fields, 1 - dx, pl.ds(ty, ny)],
            )

        return make

    def exchange(rows, far=None):
        copies = {row: [] for row, _ in rows}
        distant = []
        for i, (dx, dy) in enumerate(FAR if far is not None else ()):
            src, dst = far(dx, dy)
            distant.append(
                pltpu.make_async_remote_copy(
                    src_ref=src,
                    dst_ref=dst,
                    send_sem=far_send.at[i],
                    recv_sem=far_recv.at[i],
                    device_id=neighbour(dx, dy),
                    device_id_type=MESH,
                )
            )
            distant[-1].start()
        for i, (dx, dy) in enumerate(DIRS):
            for row, make in rows:
                src, dst = make(dx, dy)
                copies[row].append(
                    pltpu.make_async_remote_copy(
                        src_ref=src,
                        dst_ref=dst,
                        send_sem=send_sem.at[row, i],
                        recv_sem=recv_sem.at[row, i],
                        device_id=neighbour(dx, dy),
                        device_id_type=MESH,
                    )
                )
                copies[row][-1].start()
        everything = [c for group in copies.values() for c in group] + distant
        started.extend(everything)
        return everything

    def arrive(copies):
        for copy in copies:
            copy.wait_recv()

    def finish():
        disp_ref[...] = jnp.zeros_like(disp_ref)
        owned_ref[...] = jnp.zeros_like(owned_ref)
        for copy in started:
            copy.wait_send()

    far_dens = window(density, dens_win, 5, False)
    inputs = exchange(
        [
            (0, window(start, f0, 2, True)),
            (1, window(density, dens_win, 5, False)),
            (2, window(load, load_win, 1, True)),
            (3, window(solid, solid_win, 1, False)),
        ],
        far_dens,
    )

    flags = (s > 0, s < groups - 1)

    def switch(flag):
        return jnp.where(flag, 1.0, 0.0).astype(F32)

    mask_low, mask_high = switch(p > 0), switch(p < slabs - 1)
    far_low, far_high = switch(p > 1), switch(p < slabs - 2)
    locals_[0].wait()
    relax = [OMEGA / jnp.full((8, 128), st_ref[a, a, 13], F32)[0:1, :] for a in range(3)]
    tall = [-relax[a][:, 0:1] for a in range(3)]
    for ex in range(3):
        mat0[ex] = band_matrix(st_ref, ex, inner_and_ring, 24, 2, 1, flags, tall, 1.0)
    for ex in range(3):
        mat1[ex] = band_matrix(st_ref, ex, lambda r: r, 16, 1, 1, flags, None, 0.0)
    for ex in range(3):
        mat2[ex] = band_matrix(st_ref, ex, inner_and_ring, 24, 4, 2, flags, tall, 2.0)

    def triangle(distance):
        return jnp.maximum(5 - jnp.abs(distance), 0).astype(F32).astype(BF16)

    wy0_pos = band_position(lane_mod(iota((24, 96), 1), 32, 2), 5, *flags)
    wy0_ref[...] = triangle(wy0_pos - inner_and_ring(iota((24, 96), 0)))
    wy1_pos = band_position(lane_mod(iota((16, 72), 1), 24, 2), 4, *flags)
    wy1_ref[...] = triangle(wy1_pos - iota((16, 72), 0))
    wz_ref[...] = triangle(lane_mod(iota((256, 128), 0), 128, 1) - iota((256, 128), 1))
    row_y = inner_and_ring(iota((24, 128), 0))
    weight_yz = edge_weight(s * 16 + row_y, 16 * groups) * edge_weight(iota((24, 128), 1), 128)
    inv_weight = []
    for j in range(6):
        weight_x = edge_weight(jnp.full((24, 128), p * 4 + (j - 1), jnp.int32), 4 * slabs)
        inv_weight.append(1.0 / (weight_yz * weight_x))

    locals_[1].wait()
    names = owner_v[...].astype(F32)
    down, across = iota((64, 64), 0), iota((64, 64), 1)
    names_col = jnp.sum(jnp.where(down == across, names, 0.0), axis=1, keepdims=True)
    earlier = (names_col == names) & (across < down)
    rank = jnp.sum(jnp.where(earlier, 1.0, 0.0), axis=1, keepdims=True)
    code_col = names_col * 16.0 + rank
    spread = iota((64, 192), 0) == lane_mod(iota((64, 192), 1), 64, 2)
    code_row = jnp.sum(jnp.where(spread, code_col, 0.0), axis=0, keepdims=True)
    slot = iota((16 * groups, 192), 0).astype(F32)
    pick_ref[...] = jnp.where(slot == code_row, 1.0, 0.0).astype(BF16)

    for copy in locals_[2:]:
        copy.wait()
    if STAGE == 0:
        arrive(inputs)
        return finish()
    arrive(inputs)

    planes = [dens_win[j] for j in range(14)]
    for j, mask in enumerate([far_low] + [mask_low] * 4):
        planes[j] = planes[j] * mask
    for j, mask in enumerate([mask_high] * 4 + [far_high]):
        planes[9 + j] = planes[9 + j] * mask
    hfield = smooth(planes, wy0_ref, wz_ref)
    young, xphys = [], []
    for j in range(6):
        xphys.append(hfield[24 * j : 24 * j + 24] * inv_weight[j])
        solid_f = solid_win[j].astype(F32)
        young.append(EMIN + solid_f * (xphys[j] * xphys[j] * xphys[j]))
    lanes16 = iota((16, 128), 1)
    even_lane = lax.rem(lanes16, 2) == 0

    def coarsen(quarter):
        halves = [
            pair_sum(pair_sum(quarter[2 * i] + quarter[2 * i + 1], 1, 128), 0, 16) * 0.125
            for i in range(2)
        ]
        return jnp.where(even_lane, halves[0], halves[1])

    coarse[3, 1, 0:16] = coarsen([young[1 + x][0:16] for x in range(4)])
    young_in = exchange([(4, coarse_window(pl.ds(3, 1)))])
    planes = []
    for j in range(8):
        plane = f0[:, j].reshape(72, 128)
        planes.append(plane * mask_low if j < 2 else plane * mask_high if j > 5 else plane)
    relaxed = stencil_apply(planes, mat0, 24, 1)
    first = []
    for j in range(6):
        inv_young = 1.0 / young[j]
        push = jnp.concatenate(
            [relax[a] * (load_win[a, j] * inv_young) for a in range(3)], axis=0
        )
        first.append(relaxed[j] + push)

    def ends_masked(fields):
        return [fields[0] * mask_low, *fields[1:5], fields[5] * mask_high]

    s_first = stencil_apply(ends_masked(first), mat1, 16, 1)
    for a in range(3):
        coarse[a, 1, 0:16] = coarsen(
            [
                load_win[a, 1 + x, 0:16] - young[1 + x][0:16] * s_first[x][16 * a : 16 * a + 16]
                for x in range(4)
            ]
        )
    if STAGE == 1:
        arrive(young_in)
        return finish()
    coarse_in = exchange([(5, coarse_window(pl.ds(0, 3)))])
    sens_scale, out_scale = [], []
    for x in range(4):
        dens = dens_win[5 + x, 0:16]
        solid_f = solid_win[1 + x, 0:16].astype(F32)
        sens_scale.append((-3.0 * dens) * (xphys[1 + x][0:16] * xphys[1 + x][0:16]) * solid_f)
        out_scale.append(inv_weight[1 + x][0:16] / dens)
    arrive(young_in)
    arrive(coarse_in)
    if STAGE == 2:
        return finish()

    even72 = lax.rem(iota((24, 128), 1), 2) == 0
    corr_planes = []
    for plane in range(3):
        inv_cy = 1.0 / coarse[3, plane]
        both = [relax[a] * (coarse[a, plane] * inv_cy) for a in range(3)]
        if plane == 0:
            both = [v * mask_low for v in both]
        if plane == 2:
            both = [v * mask_high for v in both]
        lower = [jnp.where(even72, v, pltpu.roll(v, 1, 1)) for v in both]
        upper = [jnp.where(even72, pltpu.roll(v, 127, 1), v) for v in both]
        corr_planes.append(jnp.concatenate(lower, axis=0))
        corr_planes.append(jnp.concatenate(upper, axis=0))
    corr = stencil_apply(corr_planes, mat2, 24, 2)

    disp = [first[j] + corr[c] for j, c in enumerate((0, 1, 1, 2, 2, 3))]
    s_disp = stencil_apply(ends_masked(disp), mat1, 16, 1)
    for x in range(4):
        energy = None
        for a in range(3):
            term = disp[1 + x][24 * a : 24 * a + 16] * s_disp[x][16 * a : 16 * a + 16]
            energy = term if energy is None else energy + term
        sens_win[4 + x, 0:16] = sens_scale[x] * energy
    if STAGE == 3:
        return finish()
    sens_in = exchange([(6, window(sens_win, sens_win, 4, False, 4))])
    for x in range(4):
        for a in range(3):
            disp_ref[a, x] = disp[1 + x][24 * a : 24 * a + 16]
    arrive(sens_in)
    if STAGE == 4:
        return finish()
    planes = [sens_win[j] for j in range(12)]
    planes = [v * mask_low for v in planes[:4]] + planes[4:8] + [v * mask_high for v in planes[8:]]
    filtered = smooth(planes, wy1_ref, wz_ref) * jnp.concatenate(out_scale, axis=0)

    three = jnp.concatenate(split3(filtered), axis=0).astype(BF16)
    rows = jnp.dot(pick_ref[...], three, preferred_element_type=F32)
    for j in range(groups):
        packed[j] = rows[16 * j : 16 * j + cap]
    if STAGE == 5:
        return finish()
    gives = []
    for d in HANDOUT:
        if d >= groups:
            continue
        target = lax.rem(s + d, groups)
        gives.append(
            pltpu.make_async_remote_copy(
                src_ref=packed.at[target],
                dst_ref=owned_ref.at[s],
                send_sem=give_sem.at[d],
                recv_sem=take_sem.at[d],
                device_id=(p, target),
                device_id_type=MESH,
            )
        )
        gives[-1].start()
    owned_ref[s] = packed[s]
    arrive(gives)
    for copy in started + gives:
        copy.wait_send()


def on_device(density, solid, load, start, stencil, owner):
    slabs, groups = lax.axis_size("slab"), lax.axis_size("blk")
    cap = CAP
    hbm = pl.BlockSpec(memory_space=pltpu.HBM)
    vmem = pl.BlockSpec(memory_space=pltpu.VMEM)
    operands = (
        density,
        solid,
        load,
        start,
        stencil.transpose(1, 2, 0),
        owner.reshape(1, 64),
    )
    disp, owned = pl.pallas_call(
        functools.partial(kernel, slabs, groups, cap),
        out_shape=(
            pltpu.VMEM(load.shape, F32),
            pltpu.VMEM((groups, cap, 128), F32),
        ),
        in_specs=[hbm] * 6,
        out_specs=(vmem, vmem),
        scratch_shapes=[
            pltpu.SMEM((3, 3, 27), F32),
            pltpu.VMEM((1, 64), jnp.int32),
            pltpu.VMEM((14, 32, 128), F32),
            pltpu.VMEM((12, 24, 128), F32),
            pltpu.VMEM((3, 8, 24, 128), F32),
            pltpu.VMEM((4, 3, 24, 128), F32),
            pltpu.VMEM((3, 6, 24, 128), F32),
            pltpu.VMEM((6, 24, 128), jnp.int32),
            pltpu.VMEM((groups, cap, 128), F32),
            pltpu.VMEM((3, 216, 216), BF16),
            pltpu.VMEM((3, 144, 216), BF16),
            pltpu.VMEM((3, 216, 216), BF16),
            pltpu.VMEM((24, 96), BF16),
            pltpu.VMEM((16, 72), BF16),
            pltpu.VMEM((256, 128), BF16),
            pltpu.VMEM((16 * groups, 192), BF16),
            pltpu.SemaphoreType.DMA((6,)),
            pltpu.SemaphoreType.DMA((7, 8)),
            pltpu.SemaphoreType.DMA((7, 8)),
            pltpu.SemaphoreType.DMA((6,)),
            pltpu.SemaphoreType.DMA((6,)),
            pltpu.SemaphoreType.DMA((groups,)),
            pltpu.SemaphoreType.DMA((groups,)),
        ],
        compiler_params=pltpu.CompilerParams(
            collective_id=0, has_side_effects=True, vmem_limit_bytes=24 * 1024 * 1024
        ),
    )(*(pltpu.with_memory_space_constraint(x, pltpu.HBM) for x in operands))
    return disp, owned[None, None]


def solution(mesh):
    placed = (
        P("slab", "blk", None),
        P("slab", "blk", None),
        P(None, "slab", "blk", None),
        P(None, "slab", "blk", None),
        P(),
        P("slab", "blk", None, None),
    )
    return jax.shard_map(
        on_device,
        mesh=mesh,
        in_specs=placed,
        out_specs=(P(None, "slab", "blk", None), P("slab", "blk", None, None, None)),
        check_vma=False,
    )
```

time: 58.4 us -> 50.2 us (0.86)
  local copies, waits for them, and re-layouts: 5.94 us -> 1.3 us
  Pallas kernels: 51.4 us -> 48.2 us
    unnamed x14 -> x2, local copies, waits for them, and re-layouts: 5.94 us -> 1.3 us
    pallas_call x1, Pallas kernels: 51.4 us -> 48.2 us  [on_device(): pl.pallas_call(functools.partial(kernel, slabs, groups, cap), out_shape=(...]
where the time goes in v2:
time: 50.2 us; the launch traced here: 50.1 us
  Pallas kernels  48.2 us (96%)
  local copies, waits for them, and re-layouts  1.3 us (3%)
  between operations  0.64 us (1%)
    pallas_call x1, Pallas kernels, on_device(): pl.pallas_call(functools.partial(kernel, slabs, groups, cap), out_shape=(...  48.2 us
    unnamed x2, local copies, waits for them, and re-layouts  1.3 us

profile of v2, /device:TPU:1, one launch (start us, length us, event | category | flops | bytes accessed | tf_op | source)
XLA Modules:
  0.0 50.1 jit_solution(13191147624426707397)
XLA Ops:
  0.6 48.2 %shard_map.77 = (f32[3,4,16,128]{3,2,1,0:T(8,128)S(1)}, f32[16,10,128]{2,1,0:T(8,128)S(1)}) custom-call(f32[4,16,128]{2,1,0:T(8,128)} %density.1, s32[4,16,128]{2,1,0:T(8,128)} %solid.1, f32[3,4,16,128]{3,2,1,0:T(8,128)} %load.1, f32[3,4,16,128]{3,2,1,0:T(8,128)} %start.1, f32[3,3,27]{2,1,0:T(4,128)} %bitcast.4, s32[1,64]{1,0:T(1,128)} %bitcast.5), custom_call_target="tpu_custom_call" | custom-call | tf_op jit(solution)/shard_map/pallas_call | solution.py:498
  48.8 0.6 %copy.10 = f32[3,4,16,128]{3,2,1,0:T(8,128)} copy(f32[3,4,16,128]{3,2,1,0:T(8,128)S(1)} %get-tuple-element.8) | data formatting | bytes 196608
  49.4 0.7 %copy.8 = f32[1,1,16,10,128]{4,2,3,1,0:T(8,128)} copy(f32[1,1,16,10,128]{4,3,2,1,0:T(8,128)S(1)} %bitcast.3) | data formatting | bytes 163840

commit v3 on v2

--- a/solution.py
+++ b/solution.py
@@ -13,7 +13,6 @@
 MESH = pl.DeviceIdType.MESH
 F32 = jnp.float32
 BF16 = jnp.bfloat16
-STAGE = 99
 DIRS = ((1, 1), (1, -1), (-1, 1), (-1, -1), (0, 1), (0, -1), (1, 0), (-1, 0))
 FAR = ((2, 1), (2, -1), (-2, 1), (-2, -1), (2, 0), (-2, 0))
 HANDOUT = (12, 4, 11, 5, 13, 3, 10, 6, 14, 2, 9, 7, 8, 15, 1)
@@ -203,8 +202,27 @@
     def neighbour(dx, dy):
         return (lax.rem(p + dx + slabs, slabs), lax.rem(s + dy + groups, groups))
 
-    partners = [neighbour(dx, dy) for dx, dy in FAR + DIRS if dx != 0]
-    partners += [(p, lax.rem(s + d, groups)) for d in HANDOUT if d < groups]
+    inner = (p > 1) & (p < slabs - 2) & (s > 0) & (s < groups - 1)
+
+    def each(pairs, act, receive=False):
+        pairs = [((-dx, -dy) if receive else (dx, dy), entry) for (dx, dy), entry in pairs]
+
+        @pl.when(inner)
+        def _():
+            for _, entry in pairs:
+                act(entry)
+
+        @pl.when(jnp.logical_not(inner))
+        def _():
+            for dx, dy in FAR + DIRS:
+                group = [entry for where, entry in pairs if where == (dx, dy)]
+                if group:
+                    inside = (p + dx >= 0) & (p + dx < slabs) & (s + dy >= 0) & (s + dy < groups)
+
+                    @pl.when(inside)
+                    def _(group=group):
+                        for entry in group:
+                            act(entry)
 
     locals_ = [
         pltpu.make_async_copy(stencil, st_ref, local_sem.at[0]),
@@ -219,12 +237,34 @@
     load_win[:, :, 16:24] = jnp.zeros((3, 6, 8, 128), F32)
     solid_win[:, 16:24] = jnp.zeros((6, 8, 128), jnp.int32)
 
+    @pl.when(jnp.logical_not(inner))
+    def _():
+        f0[...] = jnp.zeros_like(f0)
+        dens_win[...] = jnp.zeros_like(dens_win)
+        load_win[...] = jnp.zeros_like(load_win)
+        solid_win[...] = jnp.zeros_like(solid_win)
+        sens_win[...] = jnp.zeros_like(sens_win)
+        coarse[...] = jnp.ones_like(coarse)
+
     barrier = pltpu.get_barrier_semaphore()
-    for partner in partners:
+
+    def greet(partner):
         pl.semaphore_signal(barrier, inc=1, device_id=partner, device_id_type=MESH)
+
+    each([((dx, dy), neighbour(dx, dy)) for dx, dy in FAR + DIRS if dx != 0], greet)
+    for d in HANDOUT:
+        if d < groups:
+            greet((p, lax.rem(s + d, groups)))
     for copy in locals_:
         copy.start()
-    pl.semaphore_wait(barrier, len(partners))
+
+    def count(flag):
+        return jnp.where(flag, jnp.int32(1), jnp.int32(0))
+
+    slabs_near = count(p > 0) + count(p < slabs - 1) + count(p > 1) + count(p < slabs - 2)
+    pl.semaphore_wait(
+        barrier, groups - 1 + slabs_near * (1 + count(s > 0) + count(s < groups - 1))
+    )
 
     started = []
 
@@ -251,48 +291,30 @@
         return make
 
     def exchange(rows, far=None):
-        copies = {row: [] for row, _ in rows}
-        distant = []
+        copies = []
+
+        def add(src, dst, dx, dy, sems):
+            copy = pltpu.make_async_remote_copy(
+                src_ref=src,
+                dst_ref=dst,
+                send_sem=sems[0],
+                recv_sem=sems[1],
+                device_id=neighbour(dx, dy),
+                device_id_type=MESH,
+            )
+            copies.append(((dx, dy), copy))
+
         for i, (dx, dy) in enumerate(FAR if far is not None else ()):
-            src, dst = far(dx, dy)
-            distant.append(
-                pltpu.make_async_remote_copy(
-                    src_ref=src,
-                    dst_ref=dst,
-                    send_sem=far_send.at[i],
-                    recv_sem=far_recv.at[i],
-                    device_id=neighbour(dx, dy),
-                    device_id_type=MESH,
-                )
-            )
-            distant[-1].start()
+            add(*far(dx, dy), dx, dy, (far_send.at[i], far_recv.at[i]))
         for i, (dx, dy) in enumerate(DIRS):
             for row, make in rows:
-                src, dst = make(dx, dy)
-                copies[row].append(
-                    pltpu.make_async_remote_copy(
-                        src_ref=src,
-                        dst_ref=dst,
-                        send_sem=send_sem.at[row, i],
-                        recv_sem=recv_sem.at[row, i],
-                        device_id=neighbour(dx, dy),
-                        device_id_type=MESH,
-                    )
-                )
-                copies[row][-1].start()
-        everything = [c for group in copies.values() for c in group] + distant
-        started.extend(everything)
-        return everything
+                add(*make(dx, dy), dx, dy, (send_sem.at[row, i], recv_sem.at[row, i]))
+        each(copies, lambda copy: copy.start())
+        started.extend(copies)
+        return copies
 
     def arrive(copies):
-        for copy in copies:
-            copy.wait_recv()
-
-    def finish():
-        disp_ref[...] = jnp.zeros_like(disp_ref)
-        owned_ref[...] = jnp.zeros_like(owned_ref)
-        for copy in started:
-            copy.wait_send()
+        each(copies, lambda copy: copy.wait_recv(), receive=True)
 
     far_dens = window(density, dens_win, 5, False)
     inputs = exchange(
@@ -311,7 +333,6 @@
         return jnp.where(flag, 1.0, 0.0).astype(F32)
 
     mask_low, mask_high = switch(p > 0), switch(p < slabs - 1)
-    far_low, far_high = switch(p > 1), switch(p < slabs - 2)
     locals_[0].wait()
     relax = [OMEGA / jnp.full((8, 128), st_ref[a, a, 13], F32)[0:1, :] for a in range(3)]
     tall = [-relax[a][:, 0:1] for a in range(3)]
@@ -349,19 +370,11 @@
     slot = iota((16 * groups, 192), 0).astype(F32)
     pick_ref[...] = jnp.where(slot == code_row, 1.0, 0.0).astype(BF16)
 
-    for copy in locals_[2:]:
+    for copy in locals_[2:6]:
         copy.wait()
-    if STAGE == 0:
-        arrive(inputs)
-        return finish()
     arrive(inputs)
 
-    planes = [dens_win[j] for j in range(14)]
-    for j, mask in enumerate([far_low] + [mask_low] * 4):
-        planes[j] = planes[j] * mask
-    for j, mask in enumerate([mask_high] * 4 + [far_high]):
-        planes[9 + j] = planes[9 + j] * mask
-    hfield = smooth(planes, wy0_ref, wz_ref)
+    hfield = smooth([dens_win[j] for j in range(14)], wy0_ref, wz_ref)
     young, xphys = [], []
     for j in range(6):
         xphys.append(hfield[24 * j : 24 * j + 24] * inv_weight[j])
@@ -379,11 +392,7 @@
 
     coarse[3, 1, 0:16] = coarsen([young[1 + x][0:16] for x in range(4)])
     young_in = exchange([(4, coarse_window(pl.ds(3, 1)))])
-    planes = []
-    for j in range(8):
-        plane = f0[:, j].reshape(72, 128)
-        planes.append(plane * mask_low if j < 2 else plane * mask_high if j > 5 else plane)
-    relaxed = stencil_apply(planes, mat0, 24, 1)
+    relaxed = stencil_apply([f0[:, j].reshape(72, 128) for j in range(8)], mat0, 24, 1)
     first = []
     for j in range(6):
         inv_young = 1.0 / young[j]
@@ -403,9 +412,6 @@
                 for x in range(4)
             ]
         )
-    if STAGE == 1:
-        arrive(young_in)
-        return finish()
     coarse_in = exchange([(5, coarse_window(pl.ds(0, 3)))])
     sens_scale, out_scale = [], []
     for x in range(4):
@@ -415,8 +421,6 @@
         out_scale.append(inv_weight[1 + x][0:16] / dens)
     arrive(young_in)
     arrive(coarse_in)
-    if STAGE == 2:
-        return finish()
 
     even72 = lax.rem(iota((24, 128), 1), 2) == 0
     corr_planes = []
@@ -441,25 +445,17 @@
             term = disp[1 + x][24 * a : 24 * a + 16] * s_disp[x][16 * a : 16 * a + 16]
             energy = term if energy is None else energy + term
         sens_win[4 + x, 0:16] = sens_scale[x] * energy
-    if STAGE == 3:
-        return finish()
     sens_in = exchange([(6, window(sens_win, sens_win, 4, False, 4))])
     for x in range(4):
         for a in range(3):
             disp_ref[a, x] = disp[1 + x][24 * a : 24 * a + 16]
     arrive(sens_in)
-    if STAGE == 4:
-        return finish()
-    planes = [sens_win[j] for j in range(12)]
-    planes = [v * mask_low for v in planes[:4]] + planes[4:8] + [v * mask_high for v in planes[8:]]
-    filtered = smooth(planes, wy1_ref, wz_ref) * jnp.concatenate(out_scale, axis=0)
+    filtered = smooth([sens_win[j] for j in range(12)], wy1_ref, wz_ref) * jnp.concatenate(out_scale, axis=0)
 
     three = jnp.concatenate(split3(filtered), axis=0).astype(BF16)
     rows = jnp.dot(pick_ref[...], three, preferred_element_type=F32)
     for j in range(groups):
         packed[j] = rows[16 * j : 16 * j + cap]
-    if STAGE == 5:
-        return finish()
     gives = []
     for d in HANDOUT:
         if d >= groups:
@@ -468,7 +464,7 @@
         gives.append(
             pltpu.make_async_remote_copy(
                 src_ref=packed.at[target],
-                dst_ref=owned_ref.at[s],
+                dst_ref=owned_ref.at[:, s],
                 send_sem=give_sem.at[d],
                 recv_sem=take_sem.at[d],
                 device_id=(p, target),
@@ -476,10 +472,25 @@
             )
         )
         gives[-1].start()
-    owned_ref[s] = packed[s]
-    arrive(gives)
-    for copy in started + gives:
+    own = pltpu.make_async_copy(packed.at[s], owned_ref.at[:, s], local_sem.at[6])
+    own.start()
+    for copy in gives:
+        copy.wait_recv()
+    own.wait()
+    for copy in gives:
         copy.wait_send()
+    each(started, lambda copy: copy.wait_send())
+
+
+def hand_out(disp_in, owned_in, disp_out, owned_out, sems):
+    copies = [
+        pltpu.make_async_copy(disp_in, disp_out, sems.at[0]),
+        pltpu.make_async_copy(owned_in, owned_out, sems.at[1]),
+    ]
+    for copy in copies:
+        copy.start()
+    for copy in copies:
+        copy.wait()
 
 
 def on_device(density, solid, load, start, stencil, owner):
@@ -499,7 +510,7 @@
         functools.partial(kernel, slabs, groups, cap),
         out_shape=(
             pltpu.VMEM(load.shape, F32),
-            pltpu.VMEM((groups, cap, 128), F32),
+            pltpu.VMEM((cap, groups, 128), F32),
         ),
         in_specs=[hbm] * 6,
         out_specs=(vmem, vmem),
@@ -520,7 +531,7 @@
             pltpu.VMEM((16, 72), BF16),
             pltpu.VMEM((256, 128), BF16),
             pltpu.VMEM((16 * groups, 192), BF16),
-            pltpu.SemaphoreType.DMA((6,)),
+            pltpu.SemaphoreType.DMA((7,)),
             pltpu.SemaphoreType.DMA((7, 8)),
             pltpu.SemaphoreType.DMA((7, 8)),
             pltpu.SemaphoreType.DMA((6,)),
@@ -532,7 +543,15 @@
             collective_id=0, has_side_effects=True, vmem_limit_bytes=24 * 1024 * 1024
         ),
     )(*(pltpu.with_memory_space_constraint(x, pltpu.HBM) for x in operands))
-    return disp, owned[None, None]
+    disp, owned = pl.pallas_call(
+        hand_out,
+        out_shape=(jax.ShapeDtypeStruct(disp.shape, F32), jax.ShapeDtypeStruct(owned.shape, F32)),
+        in_specs=[vmem, vmem],
+        out_specs=(hbm, hbm),
+        scratch_shapes=[pltpu.SemaphoreType.DMA((2,))],
+        compiler_params=pltpu.CompilerParams(vmem_limit_bytes=8 * 1024 * 1024),
+    )(*(pltpu.with_memory_space_constraint(x, pltpu.VMEM) for x in (disp, owned)))
+    return disp, owned.transpose(1, 0, 2)[None, None]
 
 
 def solution(mesh):

time: 50.2 us -> 46.8 us (0.932)
  the two profiles are of different devices: /device:TPU:1 before, /device:TPU:7 now
where the time goes in v3:
time: 46.8 us; the launch traced here: 46.7 us
  Pallas kernels  46 us (98%)
  between operations  0.64 us (1%)
    pallas_call x1, Pallas kernels, on_device(): pl.pallas_call(functools.partial(kernel, slabs, groups, cap), out_shape=(...  45.3 us

profile of v3, /device:TPU:7, one launch (start us, length us, event | category | flops | bytes accessed | tf_op | source)
XLA Modules:
  0.0 46.7 jit_solution(16797306462813280134)
XLA Ops:
  0.6 45.3 %shard_map.77 = (f32[3,4,16,128]{3,2,1,0:T(8,128)S(1)}, f32[10,16,128]{2,1,0:T(8,128)S(1)}) custom-call(f32[4,16,128]{2,1,0:T(8,128)} %density.1, s32[4,16,128]{2,1,0:T(8,128)} %solid.1, f32[3,4,16,128]{3,2,1,0:T(8,128)} %load.1, f32[3,4,16,128]{3,2,1,0:T(8,128)} %start.1, f32[3,3,27]{2,1,0:T(4,128)} %bitcast.5, s32[1,64]{1,0:T(1,128)} %bitcast.6), custom_call_target="tpu_custom_call" | custom-call | tf_op jit(solution)/shard_map/pallas_call | solution.py:509
  46.0 0.7 %shard_map.78 = (f32[3,4,16,128]{3,2,1,0:T(8,128)}, f32[10,16,128]{2,1,0:T(8,128)}) custom-call(f32[3,4,16,128]{3,2,1,0:T(8,128)S(1)} %get-tuple-element.6.disp_in, f32[10,16,128]{2,1,0:T(8,128)S(1)} %get-tuple-element.7.owned_in), custom_call_target="tpu_custom_call" | custom-call | tf_op jit(solution)/shard_map/pallas_call | solution.py:546

commit v4 on v3

--- a/solution.py
+++ b/solution.py
@@ -195,6 +195,7 @@
     far_recv,
     give_sem,
     take_sem,
+    token_sem,
 ):
     p = lax.axis_index("slab")
     s = lax.axis_index("blk")
@@ -252,9 +253,8 @@
         pl.semaphore_signal(barrier, inc=1, device_id=partner, device_id_type=MESH)
 
     each([((dx, dy), neighbour(dx, dy)) for dx, dy in FAR + DIRS if dx != 0], greet)
-    for d in HANDOUT:
-        if d < groups:
-            greet((p, lax.rem(s + d, groups)))
+    for d in (1, groups - 1):
+        greet((p, lax.rem(s + d, groups)))
     for copy in locals_:
         copy.start()
 
@@ -263,7 +263,7 @@
 
     slabs_near = count(p > 0) + count(p < slabs - 1) + count(p > 1) + count(p < slabs - 2)
     pl.semaphore_wait(
-        barrier, groups - 1 + slabs_near * (1 + count(s > 0) + count(s < groups - 1))
+        barrier, 2 + slabs_near * (1 + count(s > 0) + count(s < groups - 1))
     )
 
     started = []
@@ -316,6 +316,21 @@
     def arrive(copies):
         each(copies, lambda copy: copy.wait_recv(), receive=True)
 
+    def tell(stage):
+        reach = 2**stage
+        if 2 * reach < groups:
+            for d in (reach, groups - reach):
+                pl.semaphore_signal(
+                    token_sem.at[stage],
+                    inc=1,
+                    device_id=(p, lax.rem(s + d, groups)),
+                    device_id_type=MESH,
+                )
+
+    def hear(stage):
+        if 2 * 2**stage < groups:
+            pl.semaphore_wait(token_sem.at[stage], 2)
+
     far_dens = window(density, dens_win, 5, False)
     inputs = exchange(
         [
@@ -326,6 +341,8 @@
         ],
         far_dens,
     )
+
+    tell(0)
 
     flags = (s > 0, s < groups - 1)
 
@@ -373,6 +390,8 @@
     for copy in locals_[2:6]:
         copy.wait()
     arrive(inputs)
+    hear(0)
+    tell(1)
 
     hfield = smooth([dens_win[j] for j in range(14)], wy0_ref, wz_ref)
     young, xphys = [], []
@@ -421,6 +440,8 @@
         out_scale.append(inv_weight[1 + x][0:16] / dens)
     arrive(young_in)
     arrive(coarse_in)
+    hear(1)
+    tell(2)
 
     even72 = lax.rem(iota((24, 128), 1), 2) == 0
     corr_planes = []
@@ -450,6 +471,7 @@
         for a in range(3):
             disp_ref[a, x] = disp[1 + x][24 * a : 24 * a + 16]
     arrive(sens_in)
+    hear(2)
     filtered = smooth([sens_win[j] for j in range(12)], wy1_ref, wz_ref) * jnp.concatenate(out_scale, axis=0)
 
     three = jnp.concatenate(split3(filtered), axis=0).astype(BF16)
@@ -538,6 +560,7 @@
             pltpu.SemaphoreType.DMA((6,)),
             pltpu.SemaphoreType.DMA((groups,)),
             pltpu.SemaphoreType.DMA((groups,)),
+            pltpu.SemaphoreType.REGULAR((3,)),
         ],
         compiler_params=pltpu.CompilerParams(
             collective_id=0, has_side_effects=True, vmem_limit_bytes=24 * 1024 * 1024

time: 46.8 us -> 46.2 us (0.987)
  Pallas kernels: 46 us -> 45.1 us
    pallas_call x1, Pallas kernels: 45.3 us -> 44.4 us  [on_device(): pl.pallas_call(functools.partial(kernel, slabs, groups, cap), out_shape=(...]
where the time goes in v4:
time: 46.2 us; the launch traced here: 45.7 us
  Pallas kernels  45.1 us (98%)
  between operations  0.64 us (1%)
    pallas_call x1, Pallas kernels, on_device(): pl.pallas_call(functools.partial(kernel, slabs, groups, cap), out_shape=(...  44.4 us

profile of v4, /device:TPU:7, one launch (start us, length us, event | category | flops | bytes accessed | tf_op | source)
XLA Modules:
  0.0 45.7 jit_solution(13284478061826405371)
XLA Ops:
  0.6 44.4 %shard_map.77 = (f32[3,4,16,128]{3,2,1,0:T(8,128)S(1)}, f32[10,16,128]{2,1,0:T(8,128)S(1)}) custom-call(f32[4,16,128]{2,1,0:T(8,128)} %density.1, s32[4,16,128]{2,1,0:T(8,128)} %solid.1, f32[3,4,16,128]{3,2,1,0:T(8,128)} %load.1, f32[3,4,16,128]{3,2,1,0:T(8,128)} %start.1, f32[3,3,27]{2,1,0:T(4,128)} %bitcast.5, s32[1,64]{1,0:T(1,128)} %bitcast.6), custom_call_target="tpu_custom_call" | custom-call | tf_op jit(solution)/shard_map/pallas_call | solution.py:531
  45.0 0.7 %shard_map.78 = (f32[3,4,16,128]{3,2,1,0:T(8,128)}, f32[10,16,128]{2,1,0:T(8,128)}) custom-call(f32[3,4,16,128]{3,2,1,0:T(8,128)S(1)} %get-tuple-element.6.disp_in, f32[10,16,128]{2,1,0:T(8,128)S(1)} %get-tuple-element.7.owned_in), custom_call_target="tpu_custom_call" | custom-call | tf_op jit(solution)/shard_map/pallas_call | solution.py:569

commit v5 on v4

--- a/solution.py
+++ b/solution.py
@@ -292,6 +292,7 @@
 
     def exchange(rows, far=None):
         copies = []
+        by_row = {row: [] for row, _ in rows}
 
         def add(src, dst, dx, dy, sems):
             copy = pltpu.make_async_remote_copy(
@@ -303,18 +304,22 @@
                 device_id_type=MESH,
             )
             copies.append(((dx, dy), copy))
+            return copies[-1]
 
         for i, (dx, dy) in enumerate(FAR if far is not None else ()):
             add(*far(dx, dy), dx, dy, (far_send.at[i], far_recv.at[i]))
-        for i, (dx, dy) in enumerate(DIRS):
-            for row, make in rows:
-                add(*make(dx, dy), dx, dy, (send_sem.at[row, i], recv_sem.at[row, i]))
+        near = list(enumerate(DIRS))
+        order = [(where, entry) for where in near[:6] for entry in rows]
+        order += [(where, entry) for entry in rows for where in near[6:]]
+        for (i, (dx, dy)), (row, make) in order:
+            sems = (send_sem.at[row, i], recv_sem.at[row, i])
+            by_row[row].append(add(*make(dx, dy), dx, dy, sems))
         each(copies, lambda copy: copy.start())
         started.extend(copies)
-        return copies
+        return by_row, copies[: len(FAR)]
 
     def arrive(copies):
-        each(copies, lambda copy: copy.wait_recv(), receive=True)
+        each(copies[::-1], lambda copy: copy.wait_recv(), receive=True)
 
     def tell(stage):
         reach = 2**stage
@@ -332,16 +337,15 @@
             pl.semaphore_wait(token_sem.at[stage], 2)
 
     far_dens = window(density, dens_win, 5, False)
-    inputs = exchange(
+    inputs, far_in = exchange(
         [
+            (1, window(density, dens_win, 5, False)),
+            (3, window(solid, solid_win, 1, False)),
             (0, window(start, f0, 2, True)),
-            (1, window(density, dens_win, 5, False)),
             (2, window(load, load_win, 1, True)),
-            (3, window(solid, solid_win, 1, False)),
         ],
         far_dens,
     )
-
     tell(0)
 
     flags = (s > 0, s < groups - 1)
@@ -389,9 +393,7 @@
 
     for copy in locals_[2:6]:
         copy.wait()
-    arrive(inputs)
-    hear(0)
-    tell(1)
+    arrive(far_in + inputs[1] + inputs[3])
 
     hfield = smooth([dens_win[j] for j in range(14)], wy0_ref, wz_ref)
     young, xphys = [], []
@@ -410,8 +412,12 @@
         return jnp.where(even_lane, halves[0], halves[1])
 
     coarse[3, 1, 0:16] = coarsen([young[1 + x][0:16] for x in range(4)])
-    young_in = exchange([(4, coarse_window(pl.ds(3, 1)))])
+    young_in = exchange([(4, coarse_window(pl.ds(3, 1)))])[0][4]
+    arrive(inputs[0])
     relaxed = stencil_apply([f0[:, j].reshape(72, 128) for j in range(8)], mat0, 24, 1)
+    arrive(inputs[2])
+    hear(0)
+    tell(1)
     first = []
     for j in range(6):
         inv_young = 1.0 / young[j]
@@ -431,7 +437,7 @@
                 for x in range(4)
             ]
         )
-    coarse_in = exchange([(5, coarse_window(pl.ds(0, 3)))])
+    coarse_in = exchange([(5, coarse_window(pl.ds(0, 3)))])[0][5]
     sens_scale, out_scale = [], []
     for x in range(4):
         dens = dens_win[5 + x, 0:16]
@@ -459,14 +465,16 @@
     corr = stencil_apply(corr_planes, mat2, 24, 2)
 
     disp = [first[j] + corr[c] for j, c in enumerate((0, 1, 1, 2, 2, 3))]
-    s_disp = stencil_apply(ends_masked(disp), mat1, 16, 1)
+    corr_fine = [corr[c] for c in (0, 1, 1, 2, 2, 3)]
+    s_corr = stencil_apply(ends_masked(corr_fine), mat1, 16, 1)
+    s_disp = [s_first[x] + s_corr[x] for x in range(4)]
     for x in range(4):
         energy = None
         for a in range(3):
             term = disp[1 + x][24 * a : 24 * a + 16] * s_disp[x][16 * a : 16 * a + 16]
             energy = term if energy is None else energy + term
         sens_win[4 + x, 0:16] = sens_scale[x] * energy
-    sens_in = exchange([(6, window(sens_win, sens_win, 4, False, 4))])
+    sens_in = exchange([(6, window(sens_win, sens_win, 4, False, 4))])[0][6]
     for x in range(4):
         for a in range(3):
             disp_ref[a, x] = disp[1 + x][24 * a : 24 * a + 16]
@@ -496,12 +504,12 @@
         gives[-1].start()
     own = pltpu.make_async_copy(packed.at[s], owned_ref.at[:, s], local_sem.at[6])
     own.start()
-    for copy in gives:
-        copy.wait_recv()
     own.wait()
+    each(started, lambda copy: copy.wait_send())
     for copy in gives:
         copy.wait_send()
-    each(started, lambda copy: copy.wait_send())
+    for copy in gives[::-1]:
+        copy.wait_recv()
 
 
 def hand_out(disp_in, owned_in, disp_out, owned_out, sems):

time: 46.2 us -> 45.8 us (level)
  no operation moved by 1% of the time
where the time goes in v5:
time: 45.8 us; the launch traced here: 45.4 us
  Pallas kernels  44.8 us (98%)
  between operations  0.64 us (1%)
    pallas_call x1, Pallas kernels, on_device(): pl.pallas_call(functools.partial(kernel, slabs, groups, cap), out_shape=(...  44.1 us

profile of v5, /device:TPU:7, one launch (start us, length us, event | category | flops | bytes accessed | tf_op | source)
XLA Modules:
  0.0 45.4 jit_solution(15771997331618217452)
XLA Ops:
  0.6 44.1 %shard_map.77 = (f32[3,4,16,128]{3,2,1,0:T(8,128)S(1)}, f32[10,16,128]{2,1,0:T(8,128)S(1)}) custom-call(f32[4,16,128]{2,1,0:T(8,128)} %density.1, s32[4,16,128]{2,1,0:T(8,128)} %solid.1, f32[3,4,16,128]{3,2,1,0:T(8,128)} %load.1, f32[3,4,16,128]{3,2,1,0:T(8,128)} %start.1, f32[3,3,27]{2,1,0:T(4,128)} %bitcast.5, s32[1,64]{1,0:T(1,128)} %bitcast.6), custom_call_target="tpu_custom_call" | custom-call | tf_op jit(solution)/shard_map/pallas_call | solution.py:539
  44.7 0.7 %shard_map.78 = (f32[3,4,16,128]{3,2,1,0:T(8,128)}, f32[10,16,128]{2,1,0:T(8,128)}) custom-call(f32[3,4,16,128]{3,2,1,0:T(8,128)S(1)} %get-tuple-element.6.disp_in, f32[10,16,128]{2,1,0:T(8,128)S(1)} %get-tuple-element.7.owned_in), custom_call_target="tpu_custom_call" | custom-call | tf_op jit(solution)/shard_map/pallas_call | solution.py:577

commit v6 on v5

--- a/solution.py
+++ b/solution.py
@@ -86,17 +86,24 @@
     for plane in planes:
         high, low = split2(plane)
         parts.append(jnp.concatenate([high, low, high], axis=0).astype(BF16))
-    total = None
-    for ex in range(3):
-        right = jnp.concatenate(parts[ex : ex + count], axis=1)
-        piece = jnp.dot(mat_ref[ex], right, preferred_element_type=F32)
-        total = piece if total is None else total + piece
+    sums = [None] * count
+    for first in range(0, count + 2, 2):
+        right = jnp.concatenate(parts[first : first + 2], axis=1)
+        for ex in range(3):
+            if not any(0 <= first + k - ex < count for k in range(2)):
+                continue
+            piece = jnp.dot(mat_ref[ex], right, preferred_element_type=F32)
+            for k in range(2):
+                x = first + k - ex
+                if 0 <= x < count:
+                    part = piece[:, 128 * k : 128 * k + 128]
+                    sums[x] = part if sums[x] is None else sums[x] + part
     size = 3 * rows
     lanes = iota((size, 128), 1)
     result = []
     for x in range(count):
         down, mid, up = (
-            total[ez * size : (ez + 1) * size, x * 128 : (x + 1) * 128] for ez in range(3)
+            sums[x][ez * size : (ez + 1) * size] for ez in range(3)
         )
         down = jnp.where(lanes >= dilate, pltpu.roll(down, dilate, 1), 0.0)
         up = jnp.where(lanes < 128 - dilate, pltpu.roll(up, 128 - dilate, 1), 0.0)

time: 45.8 us -> 45.6 us (level)
  no operation moved by 1% of the time
where the time goes in v6:
time: 45.6 us; the launch traced here: 45.2 us
  Pallas kernels  44.5 us (98%)
  between operations  0.64 us (1%)
    pallas_call x1, Pallas kernels, on_device(): pl.pallas_call(functools.partial(kernel, slabs, groups, cap), out_shape=(...  43.8 us

profile of v6, /device:TPU:7, one launch (start us, length us, event | category | flops | bytes accessed | tf_op | source)
XLA Modules:
  0.0 45.2 jit_solution(7293906228027373536)
XLA Ops:
  0.6 43.8 %shard_map.77 = (f32[3,4,16,128]{3,2,1,0:T(8,128)S(1)}, f32[10,16,128]{2,1,0:T(8,128)S(1)}) custom-call(f32[4,16,128]{2,1,0:T(8,128)} %density.1, s32[4,16,128]{2,1,0:T(8,128)} %solid.1, f32[3,4,16,128]{3,2,1,0:T(8,128)} %load.1, f32[3,4,16,128]{3,2,1,0:T(8,128)} %start.1, f32[3,3,27]{2,1,0:T(4,128)} %bitcast.5, s32[1,64]{1,0:T(1,128)} %bitcast.6), custom_call_target="tpu_custom_call" | custom-call | tf_op jit(solution)/shard_map/pallas_call | solution.py:546
  44.5 0.7 %shard_map.78 = (f32[3,4,16,128]{3,2,1,0:T(8,128)}, f32[10,16,128]{2,1,0:T(8,128)}) custom-call(f32[3,4,16,128]{3,2,1,0:T(8,128)S(1)} %get-tuple-element.6.disp_in, f32[10,16,128]{2,1,0:T(8,128)S(1)} %get-tuple-element.7.owned_in), custom_call_target="tpu_custom_call" | custom-call | tf_op jit(solution)/shard_map/pallas_call | solution.py:584
